TPU v7x, 128 devices: a whole 4x4x4 slice. The times are simulated.
128 devices in a mesh: ens: 4 (over y), tile: 32 (over z, x, core).
Axes of the slice: x: 4, y: 4, z: 4, core: 2. Of those that a mesh axis runs over, the one named last changes fastest.
Arguments:
- perturbations: bfloat16 [32, 64, 32768], P('ens', None, 'tile'), may hold values from -6 to 6
- control: float32 [32, 64, 32768], P('ens', None, 'tile'), may hold values from -6 to 6
- loc_vertical: float32 [64, 64], replicated, may hold values from -0.75 to 0.75
- loc_horizontal: bfloat16 [1024, 1024], replicated, may hold values from -0.1875 to 0.1875
- obs_weight: bfloat16 [32768, 128, 128], P(('ens', 'tile')), may hold values from -0.5 to 0.5
- obs_vertical: float32 [32768, 64, 128], P(('ens', 'tile')), may hold values from -0.75 to 0.75
- innovation: float32 [32768, 128], P(('ens', 'tile')), may hold values from -6 to 6
- obs_precision: float32 [32768, 128], P(('ens', 'tile')), may hold values from 0.25 to 4
- block_column: int32 [32768], P(('ens', 'tile')), may hold values from 0 to 7
- tile_count: int32 [4096], P(('ens', 'tile')), may hold values from 7 to 8, as said below
Outputs:
- gradient: float32 [32, 64, 32768], P('ens', None, 'tile')
Inputs may be any that keep to these rules, and one draw needn't show every extreme that they name: For each destination tile the first tile_count entries of a device's 8 slots for that tile are live and the rest are padding; at most 8 blocks go from one device to one tile, and for every ens index some tile receives 8 from every device.
All inputs are finite; a program needn't handle non-finite values.
Results may differ from a plain program's by a relative error of at most 0.013.
Values may be sent and summed in bfloat16 or wider, within the bound.
A program may use at most 128 MiB of HBM per device.

v0:
```python
import math

import jax
import jax.numpy as jnp
from jax import lax
from jax.sharding import PartitionSpec as P


def on_device(
    perturbations,
    control,
    loc_vertical,
    loc_horizontal,
    obs_weight,
    obs_vertical,
    innovation,
    obs_precision,
    block_column,
    tile_count,
):
    members_dev, levels, columns = control.shape
    tile_total = lax.axis_size("tile")
    ens_total = lax.axis_size("ens")
    factor = 1.0 / math.sqrt(members_dev * ens_total - 1)
    vertical = jnp.einsum(
        "ml,klc->kmc", loc_vertical, control, precision=lax.Precision.HIGHEST
    ).astype(jnp.bfloat16)
    spread = jnp.dot(
        vertical.reshape(members_dev * levels, columns),
        loc_horizontal,
        preferred_element_type=jnp.float32,
    ).reshape(members_dev, levels, columns)
    partial_sum = jnp.sum(perturbations.astype(jnp.float32) * spread, axis=0) * factor
    state = lax.psum(partial_sum, "ens").astype(jnp.bfloat16)
    slot_count = obs_weight.shape[0]
    capacity = slot_count // tile_total
    block = obs_weight.shape[1]
    col_blocks = columns // block
    slot_index = jnp.arange(slot_count, dtype=jnp.int32)
    active = slot_index % capacity < jnp.repeat(
        tile_count, capacity, total_repeat_length=slot_count
    )
    requested = lax.all_to_all(
        block_column.reshape(tile_total, capacity), "tile", split_axis=0, concat_axis=0, tiled=True
    )
    answers = jnp.take(state.reshape(levels, col_blocks, block), requested.reshape(-1), axis=1)
    answers = answers.reshape(levels, tile_total, capacity, block)
    fetched = lax.all_to_all(answers, "tile", split_axis=1, concat_axis=1, tiled=True)
    blocks = fetched.reshape(levels, slot_count, block)
    projected = jnp.einsum("soc,lsc->slo", obs_weight, blocks, preferred_element_type=jnp.float32)
    model_obs = jnp.sum(obs_vertical * projected, axis=1)
    departure = jnp.where(
        active[:, None], obs_precision * (model_obs - innovation), jnp.float32(0.0)
    )
    weighted = (obs_vertical * departure[:, None, :]).astype(jnp.bfloat16)
    adj_blocks = jnp.einsum(
        "soc,slo->slc", obs_weight, weighted, preferred_element_type=jnp.float32
    )
    returned = lax.all_to_all(
        adj_blocks.reshape(tile_total, capacity, levels, block).astype(jnp.bfloat16),
        "tile",
        split_axis=0,
        concat_axis=0,
        tiled=True,
    ).astype(jnp.float32)
    selector = (
        requested.reshape(-1)[:, None] == jnp.arange(col_blocks, dtype=jnp.int32)[None, :]
    ).astype(jnp.float32)
    local_adj = jnp.einsum(
        "sk,slc->lkc",
        selector,
        returned.reshape(slot_count, levels, block),
        precision=lax.Precision.HIGHEST,
    ).reshape(levels, columns)
    adjoint = lax.psum(local_adj.astype(jnp.bfloat16), "ens").astype(jnp.float32)
    product_field = perturbations.astype(jnp.float32) * adjoint[None]
    back_vertical = jnp.einsum(
        "ml,kmc->klc", loc_vertical, product_field, precision=lax.Precision.HIGHEST
    ).astype(jnp.bfloat16)
    spread_back = jnp.einsum(
        "rc,dc->rd",
        back_vertical.reshape(members_dev * levels, columns),
        loc_horizontal,
        preferred_element_type=jnp.float32,
    )
    return control + factor * spread_back.reshape(members_dev, levels, columns)


def solution(mesh):
    in_specs = (
        P("ens", None, "tile"),
        P("ens", None, "tile"),
        P(),
        P(),
        P(("ens", "tile"), None, None),
        P(("ens", "tile"), None, None),
        P(("ens", "tile"), None),
        P(("ens", "tile"), None),
        P(("ens", "tile")),
        P(("ens", "tile")),
    )
    out_specs = P("ens", None, "tile")
    return jax.shard_map(
        on_device, mesh=mesh, in_specs=in_specs, out_specs=out_specs, check_vma=False
    )
```

profile of v0, /device:TPU:6, one launch (start us, length us, event | category | flops | bytes accessed | tf_op | source)
XLA Modules:
  0.0 249.6 jit_solution(8363593174624740029)
XLA Ops:
  6.5 1.5 all_to_all.12
  8.1 8.4 %all-to-all-start = ((s32[32,1,8]{2,1,0:T(1,128)}), s32[32,1,8]{2,1,0:T(1,128)S(1)}, u32[]{:S(2)}, u32[]{:S(2)}) async-start(s32[32,1,8]{2,1,0:T(1,128)} %bitcast.37), calls=%async_computation | async-start | bytes 32768 | tf_op jit(solution)/shard_map/all_to_all | solution.py:43
  16.5 3.6 %fusion.15 = bf16[8,64,1024]{2,1,0:T(8,128)(2,1)S(1)} fusion(f32[8,64,1024]{2,1,0:T(8,128)} %param.13, f32[64,64]{1,0:T(8,128)} %param.14), kind=kOutput, calls=%fused_computation.21 | convolution fusion | flops 403177472 | bytes 3162112 | tf_op jit(solution)/shard_map/ml,klc->kmc/dot_general | solution.py:25
  20.1 2.5 %fusion.6 = f32[64,1024]{1,0:T(8,128)S(1)} fusion(bf16[8,64,1024]{2,1,0:T(8,128)(2,1)} %param.12, bf16[8,64,1024]{2,1,0:T(8,128)(2,1)S(1)} %fusion.15, bf16[1024,1024]{1,0:T(8,128)(2,1)S(1)} %copy-done), kind=kOutput, calls=%fused_computation.12 | convolution fusion | flops 1075249152 | bytes 4456448 | tf_op jit(solution)/shard_map/dot_general | solution.py:28
  22.7 20.4 %all-reduce.4 = bf16[64,1024]{1,0:T(8,128)(2,1)S(1)} all-reduce(f32[64,1024]{1,0:T(8,128)S(1)} %broadcast_multiply_fusion), channel_id=1, replica_groups=mesh['ens'=4,'tile'=32] {'ens'}, use_global_device_ids=true, to_apply=%region_1.0 | all-reduce | flops 65536 | bytes 393216 | tf_op jit(solution)/shard_map/psum | solution.py:34
  43.7 0.7 reduce.57
  44.5 3.1 %gather_fusion = bf16[256,64,128]{2,1,0:T(8,128)(2,1)} fusion(bf16[64,8,128]{2,0,1:T(8,128)(2,1)S(1)} %copy_bitcast_fusion.1, s32[1024]{0:T(1024)S(1)} %pad_clamp_fusion), kind=kCustom, calls=%fused_computation | custom fusion | bytes 8389632 | tf_op jit(solution)/shard_map/jit(_take)/gather | solution.py:46
  47.6 3.8 %broadcast_select_fusion = bf16[64,32,8,128]{3,0,2,1:T(8,128)(2,1)} fusion(bf16[64,32,8,128]{3,0,2,1:T(8,128)(2,1)} %bitcast.94, pred[32,8]{1,0:T(8,128)(4,1)S(1)} %compare_and_fusion), kind=kLoop, calls=%fused_computation.8 | loop fusion | flops 2097152 | bytes 8388864 | tf_op jit(solution)/shard_map/jit(_take)/select_n | solution.py:46
  51.3 7.6 %all-to-all-start.1 = ((bf16[64,32,8,128]{3,0,2,1:T(8,128)(2,1)}), bf16[64,32,8,128]{3,0,2,1:T(8,128)(2,1)}, u32[]{:S(2)}, u32[]{:S(2)}) async-start(bf16[64,32,8,128]{3,0,2,1:T(8,128)(2,1)} %broadcast_select_fusion), calls=%async_computation.1 | async-start | bytes 8388608 | tf_op jit(solution)/shard_map/all_to_all | solution.py:48
  59.0 0.7 fusion.30
  59.7 0.7 fusion.29
  60.5 4.4 %compare_select_fusion.3 = (s32[256,1]{0,1:T(1,128)S(1)}, s32[256,1]{0,1:T(1,128)S(1)}) fusion(s32[]{:T(128)} %bitcast.29, s32[]{:T(128)} %bitcast.30, s32[]{:T(128)} %bitcast.31, s32[]{:T(128)} %bitcast.32, s32[]{:T(128)} %bitcast.33, s32[]{:T(128)} %bitcast.35, s32[]{:T(128)} %bitcast.34, s32[256,1]{0,1:T(1,128)S(1)} %bitcast.101, s32[256,1]{0,1:T(1,128)S(1)} %bitcast.100), kind=kLoop, calls=%fused_computation.65 | loop fusion | flops 3584 | bytes 4124 | tf_op jit(solution)/shard_map/jit(_take)/gather | solution.py:40
  65.0 15.5 %fusion.28 = pred[256]{0:T(512)(128)(4,1)S(1)} fusion(pred[256]{0:T(512)(128)(4,1)S(1)} %get-tuple-element.41, pred[256]{0:T(512)(128)(4,1)S(1)} %get-tuple-element.40, pred[256]{0:T(512)(128)(4,1)S(1)} %get-tuple-element.39, pred[256]{0:T(512)(128)(4,1)S(1)} %get-tuple-element.38, pred[256]{0:T(512)(128)(4,1)S(1)} %get-tuple-element.37, ...), kind=kLoop, calls=%fused_computation.76 | loop fusion | flops 10496 | bytes 8812 | tf_op jit(solution)/shard_map/lt | solution.py:40
  80.5 27.2 %all-to-all-done.1 = bf16[64,32,8,128]{3,0,2,1:T(8,128)(2,1)} async-done(((bf16[64,32,8,128]{3,0,2,1:T(8,128)(2,1)}), bf16[64,32,8,128]{3,0,2,1:T(8,128)(2,1)}, u32[]{:S(2)}, u32[]{:S(2)}) %all-to-all-start.1) | async-done | bytes 4194336 | tf_op jit(solution)/shard_map/all_to_all | solution.py:48
  107.8 12.9 %multiply_reduce_fusion = f32[256,128]{1,0:T(8,128)S(1)} fusion(f32[256,64,128]{2,1,0:T(8,128)} %param.17, bf16[64,256,128]{2,0,1:T(8,128)(2,1)} %bitcast.45, bf16[256,128,128]{2,1,0:T(8,128)(2,1)} %param.16), kind=kOutput, calls=%fused_computation.2 | convolution fusion | flops 541032448 | bytes 21102592 | tf_op jit(solution)/shard_map/soc,lsc->slo/dot_general | solution.py:50
  120.8 10.1 %fusion.5 = bf16[256,64,128]{2,1,0:T(8,128)(2,1)} fusion(bf16[256,128,128]{2,1,0:T(8,128)(2,1)} %param.16, f32[256,64,128]{2,1,0:T(8,128)} %param.17, f32[256,128]{1,0:T(8,128)S(1)} %multiply_select_fusion), kind=kOutput, calls=%fused_computation.9 | convolution fusion | flops 543162368 | bytes 21102592 | tf_op jit(solution)/shard_map/soc,slo->slc/dot_general | solution.py:56
  130.8 9.4 %all-to-all-start.2 = ((bf16[32,8,64,128]{3,2,1,0:T(8,128)(2,1)}), bf16[32,8,64,128]{3,2,1,0:T(8,128)(2,1)}, u32[]{:S(2)}, u32[]{:S(2)}) async-start(bf16[32,8,64,128]{3,2,1,0:T(8,128)(2,1)} %bitcast.93), calls=%async_computation.2 | async-start | bytes 8388608 | tf_op jit(solution)/shard_map/all_to_all | solution.py:59
  140.7 48.4 %all-to-all-done.2 = bf16[32,8,64,128]{3,2,1,0:T(8,128)(2,1)} async-done(((bf16[32,8,64,128]{3,2,1,0:T(8,128)(2,1)}), bf16[32,8,64,128]{3,2,1,0:T(8,128)(2,1)}, u32[]{:S(2)}, u32[]{:S(2)}) %all-to-all-start.2) | async-done | bytes 4194336 | tf_op jit(solution)/shard_map/all_to_all | solution.py:59
  189.0 4.5 %fusion.17 = bf16[64,128,8]{1,2,0:T(8,128)(2,1)S(1)} fusion(bf16[32,8,64,128]{3,2,1,0:T(8,128)(2,1)} %all-to-all-done.2, s32[256]{0:T(256)S(1)} %reshape.181), kind=kOutput, calls=%fused_computation.23 | convolution fusion | flops 33622016 | bytes 4326400 | tf_op jit(solution)/shard_map/sk,slc->lkc/dot_general | solution.py:69
  193.5 0.7 copy.32
  194.2 41.1 %all-reduce.3.cloned.1.call-done = bf16[64,1024]{1,0:T(8,128)(2,1)} async-done(((bf16[64,1024]{1,0:T(8,128)(2,1)}), bf16[64,1024]{1,0:T(8,128)(2,1)}) %all-reduce.3.cloned.1.call-update) | async-done | bytes 131088 | tf_op jit(solution)/shard_map/psum | solution.py:75
  235.4 0.9 convert_element_type.52
  236.3 2.2 fusion.16
  238.5 4.2 %multiply_add_fusion = f32[8,64,1024]{2,1,0:T(8,128)} fusion(f32[8,64,1024]{2,1,0:T(8,128)} %param.13, bf16[8,64,1024]{2,1,0:T(8,128)(2,1)S(1)} %fusion.16, bf16[1024,1024]{1,0:T(8,128)(2,1)S(1)} %copy-done), kind=kOutput, calls=%fused_computation.18 | convolution fusion | flops 1074790400 | bytes 7340032 | tf_op jit(solution)/shard_map/rc,dc->rd/dot_general | solution.py:80
  (29 shorter events, 1.3 us)
Async XLA Ops:
  6.5 13.6 %copy-start = (bf16[1024,1024]{1,0:T(8,128)(2,1)S(1)}, bf16[1024,1024]{1,0:T(8,128)(2,1)}, u32[]{:S(2)}) copy-start(bf16[1024,1024]{1,0:T(8,128)(2,1)} %param.15) | copy-start | bytes 6291460
  8.1 35.1 %all-to-all-start = ((s32[32,1,8]{2,1,0:T(1,128)}), s32[32,1,8]{2,1,0:T(1,128)S(1)}, u32[]{:S(2)}, u32[]{:S(2)}) async-start(s32[32,1,8]{2,1,0:T(1,128)} %bitcast.37), calls=%async_computation | async-start | bytes 32768 | tf_op jit(solution)/shard_map/all_to_all | solution.py:43
  51.3 7.6 %copy-start.2 = (s32[32]{0:T(128)S(1)}, s32[32]{0:T(128)}, u32[]{:S(2)}) copy-start(s32[32]{0:T(128)} %param.21) | copy-start | bytes 388
  51.3 9.1 %copy-start.6 = (s32[2,128]{1,0:T(2,128)S(1)}, s32[2,128]{1,0:T(2,128)}, u32[]{:S(2)}) copy-start(s32[2,128]{1,0:T(2,128)} %constant.114.clone.1) | copy-start | bytes 3076
  51.3 56.4 %all-to-all-start.1 = ((bf16[64,32,8,128]{3,0,2,1:T(8,128)(2,1)}), bf16[64,32,8,128]{3,0,2,1:T(8,128)(2,1)}, u32[]{:S(2)}, u32[]{:S(2)}) async-start(bf16[64,32,8,128]{3,0,2,1:T(8,128)(2,1)} %broadcast_select_fusion), calls=%async_computation.1 | async-start | bytes 8388608 | tf_op jit(solution)/shard_map/all_to_all | solution.py:48
  107.8 12.9 %copy-start.4 = (f32[256,128]{1,0:T(8,128)S(1)}, f32[256,128]{1,0:T(8,128)}, u32[]{:S(2)}) copy-start(f32[256,128]{1,0:T(8,128)} %param.19) | copy-start | bytes 393220
  107.8 12.9 %copy-start.5 = (f32[256,128]{1,0:T(8,128)S(1)}, f32[256,128]{1,0:T(8,128)}, u32[]{:S(2)}) copy-start(f32[256,128]{1,0:T(8,128)} %param.18) | copy-start | bytes 393220
  130.8 58.2 %all-to-all-start.2 = ((bf16[32,8,64,128]{3,2,1,0:T(8,128)(2,1)}), bf16[32,8,64,128]{3,2,1,0:T(8,128)(2,1)}, u32[]{:S(2)}, u32[]{:S(2)}) async-start(bf16[32,8,64,128]{3,2,1,0:T(8,128)(2,1)} %bitcast.93), calls=%async_computation.2 | async-start | bytes 8388608 | tf_op jit(solution)/shard_map/all_to_all | solution.py:59
  140.3 96.0 %copy-start.1 = (bf16[8,64,1024]{2,1,0:T(8,128)(2,1)S(1)}, bf16[8,64,1024]{2,1,0:T(8,128)(2,1)}, u32[]{:S(2)}) copy-start(bf16[8,64,1024]{2,1,0:T(8,128)(2,1)} %param.12) | copy-start | bytes 3145732
  140.3 96.0 %copy-start.3 = (f32[64,64]{1,0:T(8,128)S(1)}, f32[64,64]{1,0:T(8,128)}, u32[]{:S(2)}) copy-start(f32[64,64]{1,0:T(8,128)} %param.14) | copy-start | bytes 49156
  140.3 95.1 %all-reduce.3.cloned.1.call-start = ((), (), s32[]{:S(2)}) async-start(), calls=%async_computation.3 | async-start | bytes 262144 | tf_op jit(solution)/shard_map/psum | solution.py:75
Sparse Core Ops, SparseCore 0:
  194.3 40.9 all-reduce.2
where the time goes:
time: 250 us
  waiting for transfers between devices  117 us (47%)
  matrix products  39.9 us (16%)
  starting transfers between devices  25.7 us (10%)
  other arithmetic  25.6 us (10%)
  blocking collectives  20.4 us (8%)
  between operations  13.6 us (5%)
  local copies, waits for them, and re-layouts  7.44 us (3%)
    all_to_all x1, waiting for transfers between devices, on_device(): lax.all_to_all(adj_blocks.reshape(tile_total, capacity, levels, block).as...  48.4 us
    psum x1, waiting for transfers between devices, on_device(): lax.psum(local_adj.astype(jnp.bfloat16), 'ens').astype(jnp.float32)  41.1 us
    all_to_all x1, waiting for transfers between devices, on_device(): lax.all_to_all(answers, 'tile', split_axis=1, concat_axis=1, tiled=True)  27.2 us
    psum x1, blocking collectives, on_device(): state = lax.psum(partial_sum, 'ens').astype(jnp.bfloat16)  20.4 us
    lt x1, other arithmetic, on_device(): slot_index % capacity  15.5 us
    dot_general x1, matrix products, on_device(): jnp.einsum('soc,lsc->slo', obs_weight, blocks, preferred_element_type=jnp...  12.9 us
    dot_general x1, matrix products, on_device(): jnp.einsum('soc,slo->slc', obs_weight, weighted, preferred_element_type=j...  10.1 us
    all_to_all x1, starting transfers between devices, on_device(): lax.all_to_all(adj_blocks.reshape(tile_total, capacity, levels, block).as...  9.44 us
  transfers between devices with their start and end apart: 4, of which 3 were waited for; matrix products, arithmetic and copies ran while one was open for 11% of the time, Pallas kernels for 0%

commit v1 on v0

v1 whole, which is shorter than its diff:
```python
import math

import jax
import jax.numpy as jnp
from jax import lax
from jax.experimental import pallas as pl
from jax.experimental.pallas import tpu as pltpu
from jax.sharding import PartitionSpec as P

MESH = pl.DeviceIdType.MESH
F32 = jnp.float32
BF16 = jnp.bfloat16
SIDE = 4
LOADS = 8


def tile_of(z, x, c):
    return (z * SIDE + x) * 2 + c


def flat(part, c, hi, lo):
    return ((part * 2 + c) * SIDE + hi) * SIDE + lo


def exchange_kernel(
    block_ref,
    count_ref,
    prev_ref,
    last_ref,
    partial_ref,
    innov_ref,
    prec_ref,
    weight_hbm,
    vertical_hbm,
    out_ref,
    weight,
    vertical,
    sendy,
    recvy,
    state,
    chain,
    adj,
    core_in,
    total,
    half_in,
    row_in,
    plane,
    plane_in,
    unit,
    unit_b,
    unit_in,
    final,
    load_sem,
    ssem,
    rsem,
):
    e = lax.axis_index("ens")
    t = lax.axis_index("tile")
    c = t % 2
    x = (t // 2) % SIDE
    z = t // (2 * SIDE)

    slots = weight.shape[0]
    chunk = slots // LOADS
    loads = []
    for i in range(LOADS):
        at = pl.ds(i * chunk, chunk)
        for n, (src, dst) in enumerate(((weight_hbm, weight), (vertical_hbm, vertical))):
            loads.append(pltpu.make_async_copy(src.at[at], dst.at[at], load_sem.at[2 * i + n]))
    for load in loads:
        load.start()

    def along(axis, q):
        if axis == "y":
            return ((e + q) % SIDE, t)
        if axis == "x":
            return (e, tile_of(z, (x + q) % SIDE, c))
        if axis == "z":
            return (e, tile_of((z + q) % SIDE, x, c))
        return (e, tile_of(z, x, 1 - c))

    barrier = pltpu.get_barrier_semaphore()
    for axis in ("x", "y", "z"):
        for q in (1, 2, 3):
            pl.semaphore_signal(barrier, inc=1, device_id=along(axis, q), device_id_type=MESH)
    pl.semaphore_signal(barrier, inc=1, device_id=along("core", 1), device_id_type=MESH)
    pl.semaphore_wait(barrier, 10)

    used = [0]
    started = []

    def send(src, dst, axis, q=1):
        n = used[0]
        used[0] = n + 1
        copy = pltpu.make_async_remote_copy(
            src_ref=src,
            dst_ref=dst,
            send_sem=ssem.at[n],
            recv_sem=rsem.at[n],
            device_id=along(axis, q),
            device_id_type=MESH,
        )
        copy.start()
        started.append(copy)
        return copy

    hi_axis = ("z", "x")
    lo_axis = ("x", "z")
    hi = (z, x)
    lo = (x, z)

    for k in range(8):
        sendy[k] = partial_ref[:, k * 128 : (k + 1) * 128].astype(BF16)
    copies = []
    for q in (1, 2, 3):
        other = (e + q) % SIDE
        copies.append(send(sendy.at[pl.ds(2 * other, 2)], recvy.at[q - 1], "y", q))
    for copy in copies:
        copy.wait_recv()
    mine = jnp.where(e // 2 == 0, flat(0, c, z, x), flat(1, c, x, z)) * 4 + 2 * (e % 2)
    for h in range(2):
        own = partial_ref[:, pl.ds(pl.multiple_of(e * 256 + h * 128, 128), 128)]
        for q in range(3):
            own = own + recvy[q, h].astype(F32)
        state[mine + h] = own.astype(BF16)

    copies = []
    for q in (1, 2, 3):
        piece = state.at[pl.ds(mine, 2)]
        copies.append(send(piece, piece, "y", q))
    for copy in copies:
        copy.wait_recv()
    copies = []
    for p in (0, 1):
        piece = state.at[pl.ds(flat(p, c, hi[p], lo[p]) * 4, 4)]
        for q in (1, 3, 2):
            copies.append(send(piece, piece, lo_axis[p], q))
    rows = []
    cores = []

    def row_at(p, r, first=0, count=4):
        return state.at[pl.ds(flat(p, c, (hi[p] + r) % SIDE, first) * 4, count * 4)]

    for p in (0, 1):
        for q in range(3):
            copies[p * 3 + q].wait_recv()
        row = row_at(p, 0)
        rows.append([send(row, row, hi_axis[p], 1), send(row, row, hi_axis[p], 3)])
        cores.append(send(row, row, "core"))
    halves = []
    for p in (0, 1):
        rows[p][0].wait_recv()
        first = row_at(p, 3, 0, 2)
        one = send(first, first, hi_axis[p], 1)
        rows[p][1].wait_recv()
        second = row_at(p, 1, 2, 2)
        halves.append([one, send(second, second, hi_axis[p], 3)])
        for r in (3, 1):
            row = row_at(p, r)
            cores.append(send(row, row, "core"))
    for p in (0, 1):
        halves[p][0].wait_recv()
        halves[p][1].wait_recv()
        row = row_at(p, 2)
        cores.append(send(row, row, "core"))
    for copy in cores:
        copy.wait_recv()
    for load in loads:
        load.wait()

    chain[8] = jnp.zeros((64, 128), F32)

    def one_tile(j, carry):
        jc = j % 2
        jx = (j // 2) % SIDE
        jz = j // (2 * SIDE)
        f0 = flat(0, jc, jz, jx) * 4
        f1 = flat(1, jc, jx, jz) * 4 - 4
        base = pl.multiple_of(j * 8, 8)
        innov = innov_ref[pl.ds(base, 8), :]
        prec = prec_ref[pl.ds(base, 8), :]
        count = count_ref[j]
        for p in range(8):
            s = base + p
            k = block_ref[s]
            block = state[jnp.where(k < 4, f0, f1) + k]
            w = weight[s]
            v = vertical[s]
            projected = lax.dot_general(
                block, w, (((1,), (1,)), ((), ())), preferred_element_type=F32
            )
            model = jnp.sum(v * projected, axis=0, keepdims=True)
            dep = prec[p : p + 1] * (model - innov[p : p + 1])
            dep = jnp.where(p < count, dep, 0.0)
            weighted = (v * dep).astype(BF16)
            back = jnp.dot(weighted, w, preferred_element_type=F32)
            if p > 0:
                back = back + chain[prev_ref[s]]
            chain[p] = back
        for k in range(8):
            adj[(f0 if k < 4 else f1) + k] = chain[last_ref[base + k]].astype(BF16)
        return carry

    lax.fori_loop(0, 32, one_tile, 0)

    cores = []
    for r in (2, 1, 3, 0):
        for p in (0, 1):
            src = adj.at[pl.ds(flat(p, 1 - c, (hi[p] + r) % SIDE, 0) * 4, 16)]
            cores.append((p, r, send(src, core_in.at[pl.ds((p * 4 + r) * 16, 16)], "core")))
    halves = [None, None]
    for p, r, copy in cores:
        copy.wait_recv()
        src0 = flat(p, c, (hi[p] + r) % SIDE, 0) * 4
        dst0 = (p * 4 + r) * 16

        def add(i, carry):
            both = adj[src0 + i].astype(F32) + core_in[dst0 + i].astype(F32)
            total[dst0 + i] = both.astype(BF16)
            return carry

        lax.fori_loop(0, 16, add, 0)
        if r == 2:
            halves[p] = [
                send(total.at[pl.ds(dst0, 8)], half_in.at[pl.ds(p * 16, 8)], hi_axis[p], 1),
                send(total.at[pl.ds(dst0 + 8, 8)], half_in.at[pl.ds(p * 16 + 8, 8)], hi_axis[p], 3),
            ]
    rows = [None, None]
    for p in (0, 1):
        rows[p] = []
        for d, r in ((0, 1), (1, 3)):
            halves[p][d].wait_recv()
            dst0 = (p * 4 + r) * 16

            def add(i, carry):
                at = dst0 + 8 * d + i
                both = total[at].astype(F32) + half_in[p * 16 + 8 * d + i].astype(F32)
                total[at] = both.astype(BF16)
                return carry

            lax.fori_loop(0, 8, add, 0)
            rows[p].append(
                send(
                    total.at[pl.ds(dst0, 16)], row_in.at[pl.ds((p * 2 + d) * 16, 16)], hi_axis[p], r
                )
            )
    planes = [None, None]
    for p in (0, 1):
        rows[p][0].wait_recv()
        rows[p][1].wait_recv()

        def add(i, carry):
            three = (
                total[p * 64 + i].astype(F32)
                + row_in[p * 32 + i].astype(F32)
                + row_in[p * 32 + 16 + i].astype(F32)
            )
            plane[p * 16 + i] = three.astype(BF16)
            return carry

        lax.fori_loop(0, 16, add, 0)
        planes[p] = []
        for q in (1, 3, 2):
            src = plane.at[pl.ds(p * 16 + (lo[p] + q) % SIDE * 4, 4)]
            planes[p].append(
                send(src, plane_in.at[pl.ds((p * 3 + q - 1) * 4, 4)], lo_axis[p], q)
            )
    for p in (0, 1):
        for copy in planes[p]:
            copy.wait_recv()
        for i in range(4):
            both = plane[p * 16 + lo[p] * 4 + i].astype(F32)
            for q in range(3):
                both = both + plane_in[(p * 3 + q) * 4 + i].astype(F32)
            unit[p * 4 + i] = both
            unit_b[p * 4 + i] = both.astype(BF16)

    copies = []
    for q in (1, 2, 3):
        other = (e + q) % SIDE
        copies.append(send(unit_b.at[pl.ds(2 * other, 2)], unit_in.at[q - 1], "y", q))
    for copy in copies:
        copy.wait_recv()
    for h in range(2):
        both = unit[2 * e + h]
        for q in range(3):
            both = both + unit_in[q, h].astype(F32)
        final[2 * e + h] = both.astype(BF16)
    copies = []
    for q in (1, 2, 3):
        piece = final.at[pl.ds(2 * e, 2)]
        copies.append(send(piece, piece, "y", q))
    for copy in copies:
        copy.wait_recv()
    for k in range(8):
        out_ref[:, k * 128 : (k + 1) * 128] = final[k].astype(F32)
    for copy in started:
        copy.wait_send()


def exchange(partial_sum, innovation, obs_precision, obs_weight, obs_vertical, meta):
    levels, columns = partial_sum.shape
    slots, block, _ = obs_weight.shape
    smem = pl.BlockSpec(memory_space=pltpu.SMEM)
    vmem = pl.BlockSpec(memory_space=pltpu.VMEM)
    hbm = pl.BlockSpec(memory_space=pl.ANY)

    def blocks(*lead, dtype=BF16):
        return pltpu.VMEM((*lead, levels, block), dtype)

    return pl.pallas_call(
        exchange_kernel,
        out_shape=jax.ShapeDtypeStruct((levels, columns), F32),
        in_specs=[smem] * 4 + [vmem] * 3 + [hbm] * 2,
        out_specs=vmem,
        scratch_shapes=[
            pltpu.VMEM((slots, block, block), BF16),
            pltpu.VMEM((slots, levels, block), F32),
            blocks(8),
            blocks(3, 2),
            blocks(256),
            blocks(9, dtype=F32),
            blocks(256),
            blocks(128),
            blocks(128),
            blocks(32),
            blocks(64),
            blocks(32),
            blocks(24),
            blocks(8, dtype=F32),
            blocks(8),
            blocks(3, 2),
            blocks(8),
            pltpu.SemaphoreType.DMA((2 * LOADS,)),
            pltpu.SemaphoreType.DMA((64,)),
            pltpu.SemaphoreType.DMA((64,)),
        ],
        compiler_params=pltpu.CompilerParams(
            collective_id=0, has_side_effects=True, vmem_limit_bytes=48 * 1024 * 1024
        ),
    )(*meta, partial_sum, innovation, obs_precision, obs_weight, obs_vertical)


def on_device(
    perturbations,
    control,
    loc_vertical,
    loc_horizontal,
    obs_weight,
    obs_vertical,
    innovation,
    obs_precision,
    block_column,
    tile_count,
):
    members_dev, levels, columns = control.shape
    tile_total = lax.axis_size("tile")
    ens_total = lax.axis_size("ens")
    factor = 1.0 / math.sqrt(members_dev * ens_total - 1)
    vertical = jnp.einsum(
        "ml,klc->kmc", loc_vertical, control, precision=lax.Precision.HIGHEST
    ).astype(BF16)
    spread = jnp.dot(
        vertical.reshape(members_dev * levels, columns),
        loc_horizontal,
        preferred_element_type=F32,
    ).reshape(members_dev, levels, columns)
    partial_sum = jnp.sum(perturbations.astype(F32) * spread, axis=0) * factor

    slots = block_column.reshape(tile_total, 8)
    place = jnp.arange(8, dtype=jnp.int32)
    same = (slots[:, :, None] == slots[:, None, :]) & (place[:, None] > place[None, :])
    prev = jnp.max(jnp.where(same, place[None, None, :], -1), axis=2)
    prev = jnp.where(prev < 0, 8, prev).reshape(-1)
    holds = slots[:, None, :] == place[None, :, None]
    last = jnp.max(jnp.where(holds, place[None, None, :], -1), axis=2)
    last = jnp.where(last < 0, 8, last).reshape(-1)
    adjoint = exchange(
        partial_sum,
        innovation,
        obs_precision,
        obs_weight,
        obs_vertical,
        (block_column, tile_count, prev, last),
    )
    product_field = perturbations.astype(F32) * adjoint[None]
    back_vertical = jnp.einsum(
        "ml,kmc->klc", loc_vertical, product_field, precision=lax.Precision.HIGHEST
    ).astype(BF16)
    spread_back = jnp.einsum(
        "rc,dc->rd",
        back_vertical.reshape(members_dev * levels, columns),
        loc_horizontal,
        preferred_element_type=F32,
    )
    return control + factor * spread_back.reshape(members_dev, levels, columns)


def solution(mesh):
    in_specs = (
        P("ens", None, "tile"),
        P("ens", None, "tile"),
        P(),
        P(),
        P(("ens", "tile"), None, None),
        P(("ens", "tile"), None, None),
        P(("ens", "tile"), None),
        P(("ens", "tile"), None),
        P(("ens", "tile")),
        P(("ens", "tile")),
    )
    out_specs = P("ens", None, "tile")
    return jax.shard_map(
        on_device, mesh=mesh, in_specs=in_specs, out_specs=out_specs, check_vma=False
    )
```

time: 250 us -> 121 us (0.48)
  waiting for transfers between devices: 117 us -> 0 us
  Pallas kernels: 0 us -> 109 us
  matrix products: 39.9 us -> 9.7 us
  starting transfers between devices: 25.7 us -> 0 us
  other arithmetic: 25.6 us -> 0.14 us
  blocking collectives: 20.4 us -> 0 us
  between operations: 13.6 us -> 0.17 us
  local copies, waits for them, and re-layouts: 7.44 us -> 1.35 us
    pallas_call x0 -> x1, Pallas kernels: none -> 109 us  [exchange(): pl.pallas_call(exchange_kernel, out_shape=jax.ShapeDtypeStruct((levels, c...]
    all_to_all x3 -> x0, waiting for transfers between devices: 75.6 us -> none  [the longest x1 48.4 us: on_device(): lax.all_to_all(adj_blocks.reshape(tile_total, capacity, levels, block).as...]
    psum x1 -> x0, waiting for transfers between devices: 41.1 us -> none  [on_device(): lax.psum(local_adj.astype(jnp.bfloat16), 'ens').astype(jnp.float32)]
    dot_general x3 -> x0, matrix products: 27.4 us -> none  [the longest x1 12.9 us: on_device(): jnp.einsum('soc,lsc->slo', obs_weight, blocks, preferred_element_type=jnp...]
    all_to_all x3 -> x0, starting transfers between devices: 25.5 us -> none  [the longest x1 9.44 us: on_device(): lax.all_to_all(adj_blocks.reshape(tile_total, capacity, levels, block).as...]
    psum x1 -> x0, blocking collectives: 20.4 us -> none  [on_device(): state = lax.psum(partial_sum, 'ens').astype(jnp.bfloat16)]
    lt x1 -> x0, other arithmetic: 15.5 us -> none  [on_device(): slot_index % capacity]
    gather x3 -> x0, local copies, waits for them, and re-layouts: 4.5 us -> none  [the longest x1 3.06 us: on_device(): jnp.take(state.reshape(levels, col_blocks, block), requested.reshape(-1),...]
  transfers between devices with their start and end apart: 4 -> 0, of which waited for: 3 -> 0; matrix products, arithmetic and copies ran while one was open for 11% -> 0% of each run, Pallas kernels for 0% -> 0%
where the time goes in v1:
time: 121 us; the launch traced here: 120 us
  Pallas kernels  109 us (90%)
  matrix products  9.7 us (8%)
  local copies, waits for them, and re-layouts  1.35 us (1%)
    pallas_call x1, Pallas kernels, exchange(): pl.pallas_call(exchange_kernel, out_shape=jax.ShapeDtypeStruct((levels, c...  109 us
    dot_general x1, matrix products, on_device(): jnp.einsum('ml,klc->kmc', loc_vertical, control, precision=lax.Precision....  3.58 us
    dot_general x1, matrix products, on_device(): jnp.einsum('rc,dc->rd', back_vertical.reshape(members_dev * levels, colum...  2.64 us

profile of v1, /device:TPU:6, one launch (start us, length us, event | category | flops | bytes accessed | tf_op | source)
XLA Modules:
  0.0 119.9 jit_solution(4390125943247233482)
XLA Ops:
  0.0 0.0 copy-start
  0.0 0.9 eq.12
  0.9 0.1 copy.11
  1.0 0.1 select_reduce_fusion
  1.1 0.1 copy.14
  1.2 0.1 reduce_max.25
  1.3 0.1 copy.13
  1.3 0.1 reduce_max.23
  1.5 3.6 %fusion.9 = bf16[8,64,1024]{2,1,0:T(8,128)(2,1)S(1)} fusion(f32[8,64,1024]{2,1,0:T(8,128)} %param.11, f32[64,64]{1,0:T(8,128)} %param.12), kind=kOutput, calls=%fused_computation.11 | convolution fusion | flops 403177472 | bytes 3162112 | tf_op jit(solution)/shard_map/ml,klc->kmc/dot_general | solution.py:360
  5.0 0.0 copy-done
  5.1 0.0 copy-done.6
  5.1 0.0 copy-start.1
  5.1 0.0 copy-start.2
  5.1 0.0 copy-start.3
  5.1 0.0 copy-start.4
  5.1 1.3 %fusion = f32[64,1024]{1,0:T(8,128)S(1)} fusion(bf16[8,64,1024]{2,1,0:T(8,128)(2,1)S(1)} %copy-done.6, bf16[8,64,1024]{2,1,0:T(8,128)(2,1)S(1)} %fusion.9, bf16[1024,1024]{1,0:T(8,128)(2,1)S(1)} %copy-done), kind=kOutput, calls=%fused_computation.2 | convolution fusion | flops 1075249152 | bytes 4456448 | tf_op jit(solution)/shard_map/dot_general | solution.py:363
  6.4 0.0 copy-done.1
  6.4 0.0 copy-done.2
  6.5 0.0 copy-start.7
  6.5 108.5 %shard_map.100 = f32[64,1024]{1,0:T(8,128)S(1)} custom-call(s32[256]{0:T(256)S(1)} %copy-done.3, s32[32]{0:T(128)S(1)} %copy-done.4, s32[256]{0:T(256)S(1)} %get-tuple-element.8.prev_ref, s32[256]{0:T(256)S(1)} %get-tuple-element.7.last_ref, f32[64,1024]{1,0:T(8,128)S(1)} %broadcast_multiply_fusion.partial_ref, f32[256,128]{1,0:T(8,128)S(1)} %copy-done.1, ...), custom_call_target="tpu_custom_call" | custom-call | tf_op jit(solution)/shard_map/pallas_call | solution.py:311
  115.0 0.0 copy-start.5
  115.0 2.2 %fusion.10 = bf16[8,64,1024]{2,1,0:T(8,128)(2,1)S(1)} fusion(bf16[8,64,1024]{2,1,0:T(8,128)(2,1)S(1)} %copy-done.6, f32[64,1024]{1,0:T(8,128)S(1)} %shard_map.100, f32[64,64]{1,0:T(8,128)S(1)} %copy-done.7), kind=kOutput, calls=%fused_computation.12 | convolution fusion | flops 404226048 | bytes 2375680 | tf_op jit(solution)/shard_map/ml,kmc->klc/dot_general | solution.py:387
  117.2 0.0 copy-done.5
  117.2 2.6 %multiply_add_fusion = f32[8,64,1024]{2,1,0:T(8,128)} fusion(f32[8,64,1024]{2,1,0:T(8,128)S(1)} %copy-done.5, bf16[8,64,1024]{2,1,0:T(8,128)(2,1)S(1)} %fusion.10, bf16[1024,1024]{1,0:T(8,128)(2,1)S(1)} %copy-done), kind=kOutput, calls=%fused_computation.8 | convolution fusion | flops 1074790400 | bytes 7340032 | tf_op jit(solution)/shard_map/rc,dc->rd/dot_general | solution.py:390
  (7 shorter events, 0.0 us)
Async XLA Ops:
  0.0 5.0 %copy-start = (bf16[1024,1024]{1,0:T(8,128)(2,1)S(1)}, bf16[1024,1024]{1,0:T(8,128)(2,1)}, u32[]{:S(2)}) copy-start(bf16[1024,1024]{1,0:T(8,128)(2,1)} %param.13) | copy-start | bytes 6291460
  0.0 5.1 %copy-start.6 = (bf16[8,64,1024]{2,1,0:T(8,128)(2,1)S(1)}, bf16[8,64,1024]{2,1,0:T(8,128)(2,1)}, u32[]{:S(2)}) copy-start(bf16[8,64,1024]{2,1,0:T(8,128)(2,1)} %param.10) | copy-start | bytes 3145732
  5.1 1.4 %copy-start.1 = (f32[256,128]{1,0:T(8,128)S(1)}, f32[256,128]{1,0:T(8,128)}, u32[]{:S(2)}) copy-start(f32[256,128]{1,0:T(8,128)} %innov_ref.1) | copy-start | bytes 393220
  5.1 1.4 %copy-start.2 = (f32[256,128]{1,0:T(8,128)S(1)}, f32[256,128]{1,0:T(8,128)}, u32[]{:S(2)}) copy-start(f32[256,128]{1,0:T(8,128)} %prec_ref.1) | copy-start | bytes 393220
  5.1 1.4 %copy-start.3 = (s32[256]{0:T(256)S(1)}, s32[256]{0:T(256)}, u32[]{:S(2)}) copy-start(s32[256]{0:T(256)} %block_ref.1) | copy-start | bytes 3076
  5.1 1.4 %copy-start.4 = (s32[32]{0:T(128)S(1)}, s32[32]{0:T(128)}, u32[]{:S(2)}) copy-start(s32[32]{0:T(128)} %count_ref.1) | copy-start | bytes 388
  6.5 108.5 %copy-start.7 = (f32[64,64]{1,0:T(8,128)S(1)}, f32[64,64]{1,0:T(8,128)}, u32[]{:S(2)}) copy-start(f32[64,64]{1,0:T(8,128)} %param.12) | copy-start | bytes 49156
  115.0 2.2 %copy-start.5 = (f32[8,64,1024]{2,1,0:T(8,128)S(1)}, f32[8,64,1024]{2,1,0:T(8,128)}, u32[]{:S(2)}) copy-start(f32[8,64,1024]{2,1,0:T(8,128)} %param.11) | copy-start | bytes 6291460

commit v2 on v1

--- a/solution.py
+++ b/solution.py
@@ -180,22 +180,27 @@
         innov = innov_ref[pl.ds(base, 8), :]
         prec = prec_ref[pl.ds(base, 8), :]
         count = count_ref[j]
+        projs = []
         for p in range(8):
             s = base + p
             k = block_ref[s]
             block = state[jnp.where(k < 4, f0, f1) + k]
-            w = weight[s]
-            v = vertical[s]
-            projected = lax.dot_general(
-                block, w, (((1,), (1,)), ((), ())), preferred_element_type=F32
-            )
-            model = jnp.sum(v * projected, axis=0, keepdims=True)
-            dep = prec[p : p + 1] * (model - innov[p : p + 1])
-            dep = jnp.where(p < count, dep, 0.0)
-            weighted = (v * dep).astype(BF16)
-            back = jnp.dot(weighted, w, preferred_element_type=F32)
+            projs.append(lax.dot_general(
+                block, weight[s], (((1,), (1,)), ((), ())), preferred_element_type=F32
+            ))
+        models = [jnp.sum(vertical[base + p] * projs[p], axis=0, keepdims=True) for p in range(8)]
+        deps = []
+        for p in range(8):
+            dep = prec[p : p + 1] * (models[p] - innov[p : p + 1])
+            deps.append(jnp.where(p < count, dep, 0.0))
+        backs = []
+        for p in range(8):
+            weighted = (vertical[base + p] * deps[p]).astype(BF16)
+            backs.append(jnp.dot(weighted, weight[base + p], preferred_element_type=F32))
+        for p in range(8):
+            back = backs[p]
             if p > 0:
-                back = back + chain[prev_ref[s]]
+                back = back + chain[prev_ref[base + p]]
             chain[p] = back
         for k in range(8):
             adj[(f0 if k < 4 else f1) + k] = chain[last_ref[base + k]].astype(BF16)

time: 121 us -> 88.7 us (0.73)
  Pallas kernels: 109 us -> 76.1 us
    pallas_call x1, Pallas kernels: 109 us -> 76.1 us  [exchange(): pl.pallas_call(exchange_kernel, out_shape=jax.ShapeDtypeStruct((levels, c...]
where the time goes in v2:
time: 88.7 us; the launch traced here: 87.5 us
  Pallas kernels  76.1 us (86%)
  matrix products  9.7 us (11%)
  local copies, waits for them, and re-layouts  1.35 us (2%)
    pallas_call x1, Pallas kernels, exchange(): pl.pallas_call(exchange_kernel, out_shape=jax.ShapeDtypeStruct((levels, c...  76.1 us
    dot_general x1, matrix products, on_device(): jnp.einsum('ml,klc->kmc', loc_vertical, control, precision=lax.Precision....  3.58 us
    dot_general x1, matrix products, on_device(): jnp.einsum('rc,dc->rd', back_vertical.reshape(members_dev * levels, colum...  2.65 us
    dot_general x1, matrix products, on_device(): jnp.einsum('ml,kmc->klc', loc_vertical, product_field, precision=lax.Prec...  2.19 us

profile of v2, /device:TPU:6, one launch (start us, length us, event | category | flops | bytes accessed | tf_op | source)
XLA Modules:
  0.0 87.5 jit_solution(16561042626291815016)
XLA Ops:
  0.0 0.0 copy-start
  0.0 0.9 %eq.12 = s32[32,8]{1,0:T(8,128)S(1)} reshape(s32[256]{0:T(256)} %block_ref.1) | data formatting | bytes 2048 | tf_op jit(solution)/shard_map/eq | solution.py:377
  0.9 0.1 copy.11
  1.0 0.1 select_reduce_fusion
  1.1 0.1 copy.14
  1.2 0.1 reduce_max.25
  1.3 0.1 copy.13
  1.3 0.1 reduce_max.23
  1.5 3.6 %fusion.9 = bf16[8,64,1024]{2,1,0:T(8,128)(2,1)S(1)} fusion(f32[8,64,1024]{2,1,0:T(8,128)} %param.11, f32[64,64]{1,0:T(8,128)} %param.12), kind=kOutput, calls=%fused_computation.11 | convolution fusion | flops 403177472 | bytes 3162112 | tf_op jit(solution)/shard_map/ml,klc->kmc/dot_general | solution.py:365
  5.0 0.0 copy-done
  5.1 0.0 copy-done.6
  5.1 0.0 copy-start.1
  5.1 0.0 copy-start.2
  5.1 0.0 copy-start.3
  5.1 0.0 copy-start.4
  5.1 1.3 %fusion = f32[64,1024]{1,0:T(8,128)S(1)} fusion(bf16[8,64,1024]{2,1,0:T(8,128)(2,1)S(1)} %copy-done.6, bf16[8,64,1024]{2,1,0:T(8,128)(2,1)S(1)} %fusion.9, bf16[1024,1024]{1,0:T(8,128)(2,1)S(1)} %copy-done), kind=kOutput, calls=%fused_computation.2 | convolution fusion | flops 1075249152 | bytes 4456448 | tf_op jit(solution)/shard_map/dot_general | solution.py:368
  6.4 0.0 copy-done.1
  6.4 0.0 copy-done.2
  6.5 0.0 copy-start.7
  6.5 76.1 %shard_map.100 = f32[64,1024]{1,0:T(8,128)S(1)} custom-call(s32[256]{0:T(256)S(1)} %copy-done.3, s32[32]{0:T(128)S(1)} %copy-done.4, s32[256]{0:T(256)S(1)} %get-tuple-element.8.prev_ref, s32[256]{0:T(256)S(1)} %get-tuple-element.7.last_ref, f32[64,1024]{1,0:T(8,128)S(1)} %broadcast_multiply_fusion.partial_ref, f32[256,128]{1,0:T(8,128)S(1)} %copy-done.1, ...), custom_call_target="tpu_custom_call" | custom-call | tf_op jit(solution)/shard_map/pallas_call | solution.py:316
  82.6 0.0 copy-done.7
  82.6 0.0 copy-start.5
  82.6 2.2 %fusion.10 = bf16[8,64,1024]{2,1,0:T(8,128)(2,1)S(1)} fusion(bf16[8,64,1024]{2,1,0:T(8,128)(2,1)S(1)} %copy-done.6, f32[64,1024]{1,0:T(8,128)S(1)} %shard_map.100, f32[64,64]{1,0:T(8,128)S(1)} %copy-done.7), kind=kOutput, calls=%fused_computation.12 | convolution fusion | flops 404226048 | bytes 2375680 | tf_op jit(solution)/shard_map/ml,kmc->klc/dot_general | solution.py:392
  84.8 2.6 %multiply_add_fusion = f32[8,64,1024]{2,1,0:T(8,128)} fusion(f32[8,64,1024]{2,1,0:T(8,128)S(1)} %copy-done.5, bf16[8,64,1024]{2,1,0:T(8,128)(2,1)S(1)} %fusion.10, bf16[1024,1024]{1,0:T(8,128)(2,1)S(1)} %copy-done), kind=kOutput, calls=%fused_computation.8 | convolution fusion | flops 1074790400 | bytes 7340032 | tf_op jit(solution)/shard_map/rc,dc->rd/dot_general | solution.py:395
  (7 shorter events, 0.0 us)
Async XLA Ops:
  0.0 5.0 %copy-start = (bf16[1024,1024]{1,0:T(8,128)(2,1)S(1)}, bf16[1024,1024]{1,0:T(8,128)(2,1)}, u32[]{:S(2)}) copy-start(bf16[1024,1024]{1,0:T(8,128)(2,1)} %param.13) | copy-start | bytes 6291460
  0.0 5.1 %copy-start.6 = (bf16[8,64,1024]{2,1,0:T(8,128)(2,1)S(1)}, bf16[8,64,1024]{2,1,0:T(8,128)(2,1)}, u32[]{:S(2)}) copy-start(bf16[8,64,1024]{2,1,0:T(8,128)(2,1)} %param.10) | copy-start | bytes 3145732
  5.1 1.4 %copy-start.1 = (f32[256,128]{1,0:T(8,128)S(1)}, f32[256,128]{1,0:T(8,128)}, u32[]{:S(2)}) copy-start(f32[256,128]{1,0:T(8,128)} %innov_ref.1) | copy-start | bytes 393220
  5.1 1.4 %copy-start.2 = (f32[256,128]{1,0:T(8,128)S(1)}, f32[256,128]{1,0:T(8,128)}, u32[]{:S(2)}) copy-start(f32[256,128]{1,0:T(8,128)} %prec_ref.1) | copy-start | bytes 393220
  5.1 1.4 %copy-start.3 = (s32[256]{0:T(256)S(1)}, s32[256]{0:T(256)}, u32[]{:S(2)}) copy-start(s32[256]{0:T(256)} %block_ref.1) | copy-start | bytes 3076
  5.1 1.4 %copy-start.4 = (s32[32]{0:T(128)S(1)}, s32[32]{0:T(128)}, u32[]{:S(2)}) copy-start(s32[32]{0:T(128)} %count_ref.1) | copy-start | bytes 388
  6.5 76.1 %copy-start.7 = (f32[64,64]{1,0:T(8,128)S(1)}, f32[64,64]{1,0:T(8,128)}, u32[]{:S(2)}) copy-start(f32[64,64]{1,0:T(8,128)} %param.12) | copy-start | bytes 49156
  82.6 2.2 %copy-start.5 = (f32[8,64,1024]{2,1,0:T(8,128)S(1)}, f32[8,64,1024]{2,1,0:T(8,128)}, u32[]{:S(2)}) copy-start(f32[8,64,1024]{2,1,0:T(8,128)} %param.11) | copy-start | bytes 6291460

commit v3 on v0

v3 whole, which is shorter than its diff:
```python
import math

import jax
import jax.numpy as jnp
from jax import lax
from jax.experimental import pallas as pl
from jax.experimental.pallas import tpu as pltpu
from jax.sharding import PartitionSpec as P

MESH = pl.DeviceIdType.MESH
F32 = jnp.float32
BF16 = jnp.bfloat16
SIDE = 4
LOADS = 4


def tile_of(z, x, c):
    return (z * SIDE + x) * 2 + c


ORDER = (
    (0, 0), (0, 1), (0, 3), (3, 0), (1, 0), (0, 2), (3, 1), (1, 1),
    (3, 3), (1, 3), (3, 2), (1, 2), (2, 0), (2, 1), (2, 3), (2, 2),
)
ARRIVE = {
    1: ((0, 3), (0, 1), (3, 0), (1, 0)),
    3: ((0, 2),),
    5: ((3, 1), (1, 1)),
    7: ((3, 3), (1, 3)),
    9: ((3, 2), (1, 2)),
    11: ((2, 0),),
    12: ((2, 1),),
    13: ((2, 3),),
    14: ((2, 2),),
}
STEP_OF = {place: i for i, place in enumerate(ORDER)}
STEPS = len(ORDER)
LATE = (0, 1, 3, 2)


def exchange_kernel(
    block_ref,
    count_ref,
    prev_ref,
    last_ref,
    partial_ref,
    innov_ref,
    prec_ref,
    weight_hbm,
    vertical_hbm,
    out_ref,
    *scratch,
):
    rest = list(scratch)
    own = [[rest.pop(0) for _ in range(4)] for _ in range(4)]
    other = [[rest.pop(0) for _ in range(4)] for _ in range(4)]
    (
        weight,
        turned,
        vertical,
        sendy,
        recvy,
        picked,
        chain,
        adj_own,
        adj_other,
        core_in,
        total,
        half_in,
        row_in,
        plane,
        plane_in,
        unit,
        unit_b,
        unit_in,
        final,
        load_sem,
        ssem,
        rsem,
    ) = rest

    e = lax.axis_index("ens")
    t = lax.axis_index("tile")
    c = t % 2
    x = (t // 2) % SIDE
    z = t // (2 * SIDE)

    slots = weight.shape[0]
    chunk = slots // LOADS
    loads = []
    for n, (src, dst) in enumerate(((weight_hbm, weight), (vertical_hbm, vertical))):
        for i in range(LOADS):
            at = pl.ds(i * chunk, chunk)
            copy = pltpu.make_async_copy(src.at[at], dst.at[at], load_sem.at[n * LOADS + i])
            copy.start()
            loads.append(copy)

    def beside(zq, xq):
        return tile_of((z + zq) % SIDE, (x + xq) % SIDE, c)

    y_dev = {q: ((e + q) % SIDE, t) for q in (1, 2, 3)}
    hi_dev = {q: (e, jnp.where(c == 0, beside(q, 0), beside(0, q))) for q in (1, 3)}
    lo_dev = {q: (e, jnp.where(c == 0, beside(0, q), beside(q, 0))) for q in (1, 2, 3)}
    core_dev = (e, tile_of(z, x, 1 - c))

    def slot_tile(core, r, rho):
        hi = (jnp.where(core == 0, z, x) + r) % SIDE
        lo = (jnp.where(core == 0, x, z) + rho) % SIDE
        return jnp.where(core == 0, tile_of(hi, lo, 0), tile_of(lo, hi, 1))

    barrier = pltpu.get_barrier_semaphore()
    greet = [*y_dev.values(), *hi_dev.values(), *lo_dev.values(), core_dev]
    for dev in greet:
        pl.semaphore_signal(barrier, inc=1, device_id=dev, device_id_type=MESH)
    pl.semaphore_wait(barrier, len(greet))

    ways = {}

    def way(name, src, dst, dev):
        ways[name] = (len(ways), src, dst, dev)

    def copy_of(name):
        n, src, dst, dev = ways[name]
        return pltpu.make_async_remote_copy(
            src_ref=src,
            dst_ref=dst,
            send_sem=ssem.at[n],
            recv_sem=rsem.at[n],
            device_id=dev,
            device_id_type=MESH,
        )

    def go(*names):
        for name in names:
            copy_of(name).start()

    def got(*names):
        for name in names:
            copy_of(name).wait_recv()

    low, high = pl.ds(0, 4), pl.ds(4, 4)
    for i, (r, rho) in enumerate(ORDER):
        at = pl.ds(i * 8, 8)
        way(("D", i), adj_other.at[at], core_in.at[at], core_dev)
    mine = own[0][0].at[pl.ds(2 * e, 2)]
    for q in (1, 2, 3):
        way(("yr", q), sendy.at[pl.ds(2 * ((e + q) % SIDE), 2)], recvy.at[q - 1], y_dev[q])
        way(("yg", q), mine, mine, y_dev[q])
    way("A3", own[0][0], own[0][3], lo_dev[1])
    way("A1", own[0][0], own[0][1], lo_dev[3])
    way("A2a", own[0][3].at[low], own[0][2].at[low], lo_dev[1])
    way("A2b", own[0][1].at[high], own[0][2].at[high], lo_dev[3])
    for rho in range(4):
        way(("B", 3, rho), own[0][rho], own[3][rho], hi_dev[1])
        way(("B", 1, rho), own[0][rho], own[1][rho], hi_dev[3])
        way(("F", 0, rho), own[3][rho].at[low], own[2][rho].at[low], hi_dev[1])
        way(("F", 1, rho), own[1][rho].at[high], own[2][rho].at[high], hi_dev[3])
        for r in range(4):
            way(("C", r, rho), own[r][rho], other[r][rho], core_dev)

    def total_at(r, rho, first, count):
        return total.at[pl.ds(STEP_OF[r, rho] * 8 + first, count)]

    for rho in range(4):
        to_next, to_back = row_in.at[pl.ds(rho * 8, 8)], row_in.at[pl.ds(32 + rho * 8, 8)]
        way(("H", 0, rho), total_at(2, rho, 0, 4), half_in.at[pl.ds(rho * 4, 4)], hi_dev[1])
        way(("H", 1, rho), total_at(2, rho, 4, 4), half_in.at[pl.ds(16 + rho * 4, 4)], hi_dev[3])
        way(("R0u", rho), total_at(1, rho, 4, 4), row_in.at[pl.ds(rho * 8 + 4, 4)], hi_dev[1])
        way(("R0a", rho), total_at(1, rho, 0, 4), row_in.at[pl.ds(rho * 8, 4)], hi_dev[1])
        way(("R1u", rho), total_at(3, rho, 0, 4), row_in.at[pl.ds(32 + rho * 8, 4)], hi_dev[3])
        way(("R1a", rho), total_at(3, rho, 4, 4), row_in.at[pl.ds(32 + rho * 8 + 4, 4)], hi_dev[3])
    for rho in (1, 2, 3):
        way(("L", rho), plane.at[pl.ds(rho * 8, 8)], plane_in.at[pl.ds((rho - 1) * 8, 8)], lo_dev[rho])
    done = final.at[pl.ds(2 * e, 2)]
    for q in (1, 2, 3):
        way(("ur", q), unit_b.at[pl.ds(2 * ((e + q) % SIDE), 2)], unit_in.at[q - 1], y_dev[q])
        way(("ug", q), done, done, y_dev[q])

    def turn(first, count):
        def some(i, carry):
            for u in range(4):
                turned[i * 4 + u] = weight[i * 4 + u].T
            return carry

        lax.fori_loop(first // 4, (first + count) // 4, some, 0)

    for k in range(8):
        sendy[k] = partial_ref[:, k * 128 : (k + 1) * 128].astype(BF16)
    go(("yr", 1), ("yr", 3), ("yr", 2))
    for load in loads[:LOADS]:
        load.wait()
    turn(0, slots // 2)
    got(("yr", 1), ("yr", 3), ("yr", 2))
    for h in range(2):
        whole = partial_ref[:, pl.ds(pl.multiple_of(e * 256 + h * 128, 128), 128)]
        for q in range(3):
            whole = whole + recvy[q, h].astype(F32)
        own[0][0][2 * e + h] = whole.astype(BF16)
    go(("yg", 1), ("yg", 3), ("yg", 2))
    turn(slots // 2, slots // 2)
    got(("yg", 1), ("yg", 3), ("yg", 2))
    go("A3", "A1", ("B", 3, 0), ("B", 1, 0), ("C", 0, 0))
    for load in loads[LOADS:]:
        load.wait()
    for f in range(2):
        chain[f * 9 + 8] = jnp.zeros((64, 128), F32)

    def arrived(r, rho):
        if r == 0 and rho == 2:
            got("A2a", "A2b")
        elif r == 0:
            got("A%d" % rho)
            go("A2a" if rho == 3 else "A2b")
        elif r == 2:
            got(("F", 0, rho), ("F", 1, rho))
        else:
            got(("B", r, rho))
            go(("F", 0 if r == 3 else 1, rho))
        if r == 0:
            go(("B", 3, rho), ("B", 1, rho))
        go(("C", r, rho))

    def event(i):
        for place in ARRIVE.get(i, ()):
            arrived(*place)
        if i == 13:
            for rho in LATE:
                go(("R0u", rho), ("R1u", rho))
        if i >= 2 and ORDER[i - 2][0] == 2:
            rho = ORDER[i - 2][1]
            go(("H", 0, rho), ("H", 1, rho))
        if i < STEPS:
            r, rho = ORDER[i]
            got(("C", r, rho))
            for f, refs in ((0, own), (1, other)):
                base = slot_tile(c if f == 0 else 1 - c, r, rho) * 8
                for p in range(8):
                    picked[f * 8 + p] = refs[r][rho][block_ref[base + p]]

    def dispatch(i, first, last):
        if last - first == 1:
            event(first)
            return
        middle = (first + last) // 2

        @pl.when(i < middle)
        def _():
            dispatch(i, first, middle)

        @pl.when(i >= middle)
        def _():
            dispatch(i, middle, last)

    def add_core(i):
        pltpu.make_async_remote_copy(
            src_ref=adj_other.at[pl.ds(i * 8, 8)],
            dst_ref=core_in.at[pl.ds(i * 8, 8)],
            send_sem=ssem.at[i],
            recv_sem=rsem.at[i],
            device_id=core_dev,
            device_id_type=MESH,
        ).wait_recv()
        for k in range(8):
            both = adj_own[i * 8 + k].astype(F32) + core_in[i * 8 + k].astype(F32)
            total[i * 8 + k] = both.astype(BF16)

    def step(i, carry):
        @pl.when(i >= 2)
        def _():
            add_core(i - 2)

        dispatch(i, 0, STEPS)
        r, rho = jnp.int32(0), jnp.int32(0)
        for n, (rn, rhon) in enumerate(ORDER):
            r = jnp.where(i == n, rn, r)
            rho = jnp.where(i == n, rhon, rho)
        pairs = []
        for f in range(2):
            tile = slot_tile(c if f == 0 else 1 - c, r, rho)
            pairs.append((f, tile, pl.multiple_of(tile * 8, 8)))
        both = [(f, tile, base, p) for f, tile, base in pairs for p in range(8)]
        innov = [innov_ref[pl.ds(base, 8), :] for _, _, base in pairs]
        prec = [prec_ref[pl.ds(base, 8), :] for _, _, base in pairs]
        projs = [
            jnp.dot(picked[f * 8 + p], turned[base + p], preferred_element_type=F32)
            for f, tile, base, p in both
        ]
        deps = []
        for f, tile, base, p in both:
            model = jnp.sum(vertical[base + p] * projs[f * 8 + p], axis=0, keepdims=True)
            dep = prec[f][p : p + 1] * (model - innov[f][p : p + 1])
            deps.append(jnp.where(p < count_ref[tile], dep, 0.0))
        backs = []
        for f, tile, base, p in both:
            weighted = (vertical[base + p] * deps[f * 8 + p]).astype(BF16)
            backs.append(jnp.dot(weighted, weight[base + p], preferred_element_type=F32))
        for f, tile, base, p in both:
            back = backs[f * 8 + p]
            if p > 0:
                back = back + chain[f * 9 + prev_ref[base + p]]
            chain[f * 9 + p] = back
        for f, tile, base in pairs:
            into = adj_own if f == 0 else adj_other
            for k in range(8):
                into[i * 8 + k] = chain[f * 9 + last_ref[base + k]].astype(BF16)
        pltpu.make_async_remote_copy(
            src_ref=adj_other.at[pl.ds(i * 8, 8)],
            dst_ref=core_in.at[pl.ds(i * 8, 8)],
            send_sem=ssem.at[i],
            recv_sem=rsem.at[i],
            device_id=core_dev,
            device_id_type=MESH,
        ).start()
        return carry

    lax.fori_loop(0, STEPS, step, 0)

    for i in (STEPS, STEPS + 1):
        add_core(i - 2)
        event(i)
    for rho in LATE:
        for d, r, first, name in ((0, 1, 0, "R0a"), (1, 3, 4, "R1a")):
            got(("H", d, rho))
            for b in range(4):
                at = STEP_OF[r, rho] * 8 + first + b
                sum_ = total[at].astype(F32) + half_in[d * 16 + rho * 4 + b].astype(F32)
                total[at] = sum_.astype(BF16)
            go((name, rho))
    for rho in (1, 3, 2, 0):
        got(("R0u", rho), ("R0a", rho), ("R1u", rho), ("R1a", rho))
        for k in range(8):
            sum_ = (
                total[STEP_OF[0, rho] * 8 + k].astype(F32)
                + row_in[rho * 8 + k].astype(F32)
                + row_in[32 + rho * 8 + k].astype(F32)
            )
            if rho == 0:
                unit[k] = sum_
            else:
                plane[rho * 8 + k] = sum_.astype(BF16)
        if rho != 0:
            go(("L", rho))
    got(("L", 1), ("L", 3), ("L", 2))
    for k in range(8):
        sum_ = unit[k]
        for q in range(3):
            sum_ = sum_ + plane_in[q * 8 + k].astype(F32)
        unit[k] = sum_
        unit_b[k] = sum_.astype(BF16)

    go(("ur", 1), ("ur", 3), ("ur", 2))
    got(("ur", 1), ("ur", 3), ("ur", 2))
    for h in range(2):
        sum_ = unit[2 * e + h]
        for q in range(3):
            sum_ = sum_ + unit_in[q, h].astype(F32)
        final[2 * e + h] = sum_.astype(BF16)
    go(("ug", 1), ("ug", 3), ("ug", 2))
    got(("ug", 1), ("ug", 3), ("ug", 2))
    for k in range(8):
        out_ref[:, k * 128 : (k + 1) * 128] = final[k].astype(F32)
    for name in ways:
        copy_of(name).wait_send()


def exchange(partial_sum, innovation, obs_precision, obs_weight, obs_vertical, meta):
    levels, columns = partial_sum.shape
    slots, block, _ = obs_weight.shape
    smem = pl.BlockSpec(memory_space=pltpu.SMEM)
    vmem = pl.BlockSpec(memory_space=pltpu.VMEM)
    hbm = pl.BlockSpec(memory_space=pl.ANY)

    def blocks(*lead, dtype=BF16):
        return pltpu.VMEM((*lead, levels, block), dtype)

    return pl.pallas_call(
        exchange_kernel,
        out_shape=jax.ShapeDtypeStruct((levels, columns), F32),
        in_specs=[smem] * 4 + [vmem] * 3 + [hbm] * 2,
        out_specs=vmem,
        scratch_shapes=[blocks(8) for _ in range(32)]
        + [
            pltpu.VMEM((slots, block, block), BF16),
            pltpu.VMEM((slots, block, block), BF16),
            pltpu.VMEM((slots, levels, block), F32),
            blocks(8),
            blocks(3, 2),
            blocks(16),
            blocks(18, dtype=F32),
            blocks(128),
            blocks(128),
            blocks(128),
            blocks(128),
            blocks(32),
            blocks(64),
            blocks(32),
            blocks(24),
            blocks(8, dtype=F32),
            blocks(8),
            blocks(3, 2),
            blocks(8),
            pltpu.SemaphoreType.DMA((2 * LOADS,)),
            pltpu.SemaphoreType.DMA((112,)),
            pltpu.SemaphoreType.DMA((112,)),
        ],
        compiler_params=pltpu.CompilerParams(
            collective_id=0, has_side_effects=True, vmem_limit_bytes=52 * 1024 * 1024
        ),
    )(*meta, partial_sum, innovation, obs_precision, obs_weight, obs_vertical)


def on_device(
    perturbations,
    control,
    loc_vertical,
    loc_horizontal,
    obs_weight,
    obs_vertical,
    innovation,
    obs_precision,
    block_column,
    tile_count,
):
    members_dev, levels, columns = control.shape
    tile_total = lax.axis_size("tile")
    ens_total = lax.axis_size("ens")
    factor = 1.0 / math.sqrt(members_dev * ens_total - 1)
    vertical = jnp.einsum(
        "ml,klc->kmc", loc_vertical, control, precision=lax.Precision.HIGHEST
    ).astype(BF16)
    spread = jnp.dot(
        vertical.reshape(members_dev * levels, columns),
        loc_horizontal,
        preferred_element_type=F32,
    ).reshape(members_dev, levels, columns)
    partial_sum = jnp.sum(perturbations.astype(F32) * spread, axis=0) * factor

    slots = block_column.reshape(tile_total, 8)
    place = jnp.arange(8, dtype=jnp.int32)
    same = (slots[:, :, None] == slots[:, None, :]) & (place[:, None] > place[None, :])
    prev = jnp.max(jnp.where(same, place[None, None, :], -1), axis=2)
    prev = jnp.where(prev < 0, 8, prev).reshape(-1)
    holds = slots[:, None, :] == place[None, :, None]
    last = jnp.max(jnp.where(holds, place[None, None, :], -1), axis=2)
    last = jnp.where(last < 0, 8, last).reshape(-1)
    adjoint = exchange(
        partial_sum,
        innovation,
        obs_precision,
        obs_weight,
        obs_vertical,
        (block_column, tile_count, prev, last),
    )
    product_field = perturbations.astype(F32) * adjoint[None]
    back_vertical = jnp.einsum(
        "ml,kmc->klc", loc_vertical, product_field, precision=lax.Precision.HIGHEST
    ).astype(BF16)
    spread_back = jnp.einsum(
        "rc,dc->rd",
        back_vertical.reshape(members_dev * levels, columns),
        loc_horizontal,
        preferred_element_type=F32,
    )
    return control + factor * spread_back.reshape(members_dev, levels, columns)


def solution(mesh):
    in_specs = (
        P("ens", None, "tile"),
        P("ens", None, "tile"),
        P(),
        P(),
        P(("ens", "tile"), None, None),
        P(("ens", "tile"), None, None),
        P(("ens", "tile"), None),
        P(("ens", "tile"), None),
        P(("ens", "tile")),
        P(("ens", "tile")),
    )
    out_specs = P("ens", None, "tile")
    return jax.shard_map(
        on_device, mesh=mesh, in_specs=in_specs, out_specs=out_specs, check_vma=False
    )
```

time: 250 us -> 72 us (0.29)
  waiting for transfers between devices: 117 us -> 0 us
  Pallas kernels: 0 us -> 60.5 us
  matrix products: 39.9 us -> 9.7 us
  starting transfers between devices: 25.7 us -> 0 us
  other arithmetic: 25.6 us -> 0.14 us
  blocking collectives: 20.4 us -> 0 us
  between operations: 13.6 us -> 0.17 us
  local copies, waits for them, and re-layouts: 7.44 us -> 1.35 us
    all_to_all x3 -> x0, waiting for transfers between devices: 75.6 us -> none  [the longest x1 48.4 us: on_device(): lax.all_to_all(adj_blocks.reshape(tile_total, capacity, levels, block).as...]
    pallas_call x0 -> x1, Pallas kernels: none -> 60.5 us  [exchange(): pl.pallas_call(exchange_kernel, out_shape=jax.ShapeDtypeStruct((levels, c...]
    psum x1 -> x0, waiting for transfers between devices: 41.1 us -> none  [on_device(): lax.psum(local_adj.astype(jnp.bfloat16), 'ens').astype(jnp.float32)]
    dot_general x3 -> x0, matrix products: 27.4 us -> none  [the longest x1 12.9 us: on_device(): jnp.einsum('soc,lsc->slo', obs_weight, blocks, preferred_element_type=jnp...]
    all_to_all x3 -> x0, starting transfers between devices: 25.5 us -> none  [the longest x1 9.44 us: on_device(): lax.all_to_all(adj_blocks.reshape(tile_total, capacity, levels, block).as...]
    psum x1 -> x0, blocking collectives: 20.4 us -> none  [on_device(): state = lax.psum(partial_sum, 'ens').astype(jnp.bfloat16)]
    lt x1 -> x0, other arithmetic: 15.5 us -> none  [on_device(): slot_index % capacity]
    gather x3 -> x0, local copies, waits for them, and re-layouts: 4.5 us -> none  [the longest x1 3.06 us: on_device(): jnp.take(state.reshape(levels, col_blocks, block), requested.reshape(-1),...]
  transfers between devices with their start and end apart: 4 -> 0, of which waited for: 3 -> 0; matrix products, arithmetic and copies ran while one was open for 11% -> 0% of each run, Pallas kernels for 0% -> 0%
where the time goes in v3:
time: 72 us; the launch traced here: 71.8 us
  Pallas kernels  60.5 us (84%)
  matrix products  9.7 us (13%)
  local copies, waits for them, and re-layouts  1.35 us (2%)
    pallas_call x1, Pallas kernels, exchange(): pl.pallas_call(exchange_kernel, out_shape=jax.ShapeDtypeStruct((levels, c...  60.5 us
    dot_general x1, matrix products, on_device(): jnp.einsum('ml,klc->kmc', loc_vertical, control, precision=lax.Precision....  3.58 us
    dot_general x1, matrix products, on_device(): jnp.einsum('rc,dc->rd', back_vertical.reshape(members_dev * levels, colum...  2.65 us
    dot_general x1, matrix products, on_device(): jnp.einsum('ml,kmc->klc', loc_vertical, product_field, precision=lax.Prec...  2.19 us

profile of v3, /device:TPU:6, one launch (start us, length us, event | category | flops | bytes accessed | tf_op | source)
XLA Modules:
  0.0 71.8 jit_solution(3546447714754758339)
XLA Ops:
  0.0 0.0 copy-start
  0.0 0.9 %eq.12 = s32[32,8]{1,0:T(8,128)S(1)} reshape(s32[256]{0:T(256)} %block_ref.1) | data formatting | bytes 2048 | tf_op jit(solution)/shard_map/eq | solution.py:440
  0.9 0.1 copy.11
  1.0 0.1 select_reduce_fusion
  1.1 0.1 copy.14
  1.2 0.1 reduce_max.25
  1.3 0.1 copy.13
  1.3 0.1 reduce_max.23
  1.5 3.6 %fusion.9 = bf16[8,64,1024]{2,1,0:T(8,128)(2,1)S(1)} fusion(f32[8,64,1024]{2,1,0:T(8,128)} %param.11, f32[64,64]{1,0:T(8,128)} %param.12), kind=kOutput, calls=%fused_computation.11 | convolution fusion | flops 403177472 | bytes 3162112 | tf_op jit(solution)/shard_map/ml,klc->kmc/dot_general | solution.py:428
  5.0 0.0 copy-done
  5.1 0.0 copy-done.6
  5.1 0.0 copy-start.1
  5.1 0.0 copy-start.2
  5.1 0.0 copy-start.3
  5.1 0.0 copy-start.4
  5.1 1.3 %fusion = f32[64,1024]{1,0:T(8,128)S(1)} fusion(bf16[8,64,1024]{2,1,0:T(8,128)(2,1)S(1)} %copy-done.6, bf16[8,64,1024]{2,1,0:T(8,128)(2,1)S(1)} %fusion.9, bf16[1024,1024]{1,0:T(8,128)(2,1)S(1)} %copy-done), kind=kOutput, calls=%fused_computation.2 | convolution fusion | flops 1075249152 | bytes 4456448 | tf_op jit(solution)/shard_map/dot_general | solution.py:431
  6.4 0.0 copy-done.1
  6.4 0.0 copy-done.2
  6.5 0.0 copy-done.3
  6.5 0.0 copy-start.7
  6.5 60.5 %shard_map.100 = f32[64,1024]{1,0:T(8,128)S(1)} custom-call(s32[256]{0:T(256)S(1)} %copy-done.3, s32[32]{0:T(128)S(1)} %copy-done.4, s32[256]{0:T(256)S(1)} %get-tuple-element.8.prev_ref, s32[256]{0:T(256)S(1)} %get-tuple-element.7.last_ref, f32[64,1024]{1,0:T(8,128)S(1)} %broadcast_multiply_fusion.partial_ref, f32[256,128]{1,0:T(8,128)S(1)} %copy-done.1, ...), custom_call_target="tpu_custom_call" | custom-call | tf_op jit(solution)/shard_map/pallas_call | solution.py:376
  67.0 0.0 copy-start.5
  67.0 2.2 %fusion.10 = bf16[8,64,1024]{2,1,0:T(8,128)(2,1)S(1)} fusion(bf16[8,64,1024]{2,1,0:T(8,128)(2,1)S(1)} %copy-done.6, f32[64,1024]{1,0:T(8,128)S(1)} %shard_map.100, f32[64,64]{1,0:T(8,128)S(1)} %copy-done.7), kind=kOutput, calls=%fused_computation.12 | convolution fusion | flops 404226048 | bytes 2375680 | tf_op jit(solution)/shard_map/ml,kmc->klc/dot_general | solution.py:455
  69.2 2.6 %multiply_add_fusion = f32[8,64,1024]{2,1,0:T(8,128)} fusion(f32[8,64,1024]{2,1,0:T(8,128)S(1)} %copy-done.5, bf16[8,64,1024]{2,1,0:T(8,128)(2,1)S(1)} %fusion.10, bf16[1024,1024]{1,0:T(8,128)(2,1)S(1)} %copy-done), kind=kOutput, calls=%fused_computation.8 | convolution fusion | flops 1074790400 | bytes 7340032 | tf_op jit(solution)/shard_map/rc,dc->rd/dot_general | solution.py:458
  (7 shorter events, 0.0 us)
Async XLA Ops:
  0.0 5.0 %copy-start = (bf16[1024,1024]{1,0:T(8,128)(2,1)S(1)}, bf16[1024,1024]{1,0:T(8,128)(2,1)}, u32[]{:S(2)}) copy-start(bf16[1024,1024]{1,0:T(8,128)(2,1)} %param.13) | copy-start | bytes 6291460
  0.0 5.1 %copy-start.6 = (bf16[8,64,1024]{2,1,0:T(8,128)(2,1)S(1)}, bf16[8,64,1024]{2,1,0:T(8,128)(2,1)}, u32[]{:S(2)}) copy-start(bf16[8,64,1024]{2,1,0:T(8,128)(2,1)} %param.10) | copy-start | bytes 3145732
  5.1 1.4 %copy-start.1 = (f32[256,128]{1,0:T(8,128)S(1)}, f32[256,128]{1,0:T(8,128)}, u32[]{:S(2)}) copy-start(f32[256,128]{1,0:T(8,128)} %innov_ref.1) | copy-start | bytes 393220
  5.1 1.4 %copy-start.2 = (f32[256,128]{1,0:T(8,128)S(1)}, f32[256,128]{1,0:T(8,128)}, u32[]{:S(2)}) copy-start(f32[256,128]{1,0:T(8,128)} %prec_ref.1) | copy-start | bytes 393220
  5.1 1.4 %copy-start.3 = (s32[256]{0:T(256)S(1)}, s32[256]{0:T(256)}, u32[]{:S(2)}) copy-start(s32[256]{0:T(256)} %block_ref.1) | copy-start | bytes 3076
  5.1 1.4 %copy-start.4 = (s32[32]{0:T(128)S(1)}, s32[32]{0:T(128)}, u32[]{:S(2)}) copy-start(s32[32]{0:T(128)} %count_ref.1) | copy-start | bytes 388
  6.5 60.5 %copy-start.7 = (f32[64,64]{1,0:T(8,128)S(1)}, f32[64,64]{1,0:T(8,128)}, u32[]{:S(2)}) copy-start(f32[64,64]{1,0:T(8,128)} %param.12) | copy-start | bytes 49156
  67.0 2.2 %copy-start.5 = (f32[8,64,1024]{2,1,0:T(8,128)S(1)}, f32[8,64,1024]{2,1,0:T(8,128)}, u32[]{:S(2)}) copy-start(f32[8,64,1024]{2,1,0:T(8,128)} %param.11) | copy-start | bytes 6291460

commit v4 on v3

--- a/solution.py
+++ b/solution.py
@@ -1,3 +1,4 @@
+import functools
 import math
 
 import jax
@@ -39,13 +40,15 @@
 
 
 def exchange_kernel(
+    factor,
     block_ref,
     count_ref,
-    prev_ref,
-    last_ref,
-    partial_ref,
+    loc_vertical_ref,
     innov_ref,
     prec_ref,
+    pert_hbm,
+    control_hbm,
+    horizontal_hbm,
     weight_hbm,
     vertical_hbm,
     out_ref,
@@ -55,6 +58,12 @@
     own = [[rest.pop(0) for _ in range(4)] for _ in range(4)]
     other = [[rest.pop(0) for _ in range(4)] for _ in range(4)]
     (
+        pert,
+        control,
+        horizontal,
+        localized,
+        prev_ref,
+        last_ref,
         weight,
         turned,
         vertical,
@@ -85,6 +94,13 @@
     x = (t // 2) % SIDE
     z = t // (2 * SIDE)
 
+    first_loads = []
+    for n, (src, dst) in enumerate(
+        ((control_hbm, control), (horizontal_hbm, horizontal), (pert_hbm, pert))
+    ):
+        copy = pltpu.make_async_copy(src, dst, load_sem.at[2 * LOADS + n])
+        copy.start()
+        first_loads.append(copy)
     slots = weight.shape[0]
     chunk = slots // LOADS
     loads = []
@@ -112,8 +128,6 @@
     greet = [*y_dev.values(), *hi_dev.values(), *lo_dev.values(), core_dev]
     for dev in greet:
         pl.semaphore_signal(barrier, inc=1, device_id=dev, device_id_type=MESH)
-    pl.semaphore_wait(barrier, len(greet))
-
     ways = {}
 
     def way(name, src, dst, dev):
@@ -144,7 +158,7 @@
         way(("D", i), adj_other.at[at], core_in.at[at], core_dev)
     mine = own[0][0].at[pl.ds(2 * e, 2)]
     for q in (1, 2, 3):
-        way(("yr", q), sendy.at[pl.ds(2 * ((e + q) % SIDE), 2)], recvy.at[q - 1], y_dev[q])
+        way(("yr", q), sendy.at[q - 1], recvy.at[q - 1], y_dev[q])
         way(("yg", q), mine, mine, y_dev[q])
     way("A3", own[0][0], own[0][3], lo_dev[1])
     way("A1", own[0][0], own[0][1], lo_dev[3])
@@ -184,22 +198,71 @@
 
         lax.fori_loop(first // 4, (first + count) // 4, some, 0)
 
-    for k in range(8):
-        sendy[k] = partial_ref[:, k * 128 : (k + 1) * 128].astype(BF16)
-    go(("yr", 1), ("yr", 3), ("yr", 2))
+    def tables(j, carry):
+        base = j * 8
+        columns = [block_ref[base + p] for p in range(8)]
+        for p in range(8):
+            before = jnp.int32(8)
+            for n in range(p):
+                before = jnp.where(columns[n] == columns[p], n, before)
+            prev_ref[base + p] = before
+        for k in range(8):
+            latest = jnp.int32(8)
+            for n in range(8):
+                latest = jnp.where(columns[n] == k, n, latest)
+            last_ref[base + k] = latest
+        return carry
+
+    lv = loc_vertical_ref[...]
+    head = lv.astype(BF16)
+    heads = jnp.concatenate([head, (lv - head.astype(F32)).astype(BF16)], axis=0)
+    first_loads[0].wait()
+
+    def one_member(k, carry):
+        field = control[k]
+        field_head = field.astype(BF16)
+        field_rest = (field - field_head.astype(F32)).astype(BF16)
+        two = jnp.dot(heads, field_head, preferred_element_type=F32)
+        sum_ = two[:64] + two[64:] + jnp.dot(head, field_rest, preferred_element_type=F32)
+        localized[pl.ds(pl.multiple_of(k * 64, 64), 64), :] = sum_.astype(BF16)
+        return carry
+
+    lax.fori_loop(0, 8, one_member, 0)
+    for load in first_loads[1:]:
+        load.wait()
+
+    def increment(q):
+        at = pl.ds(pl.multiple_of((e + q) % SIDE * 256, 256), 256)
+        spread = jnp.dot(localized[...], horizontal[:, at], preferred_element_type=F32)
+        sum_ = pert[0, :, at].astype(F32) * spread[:64]
+        for k in range(1, 8):
+            sum_ = sum_ + pert[k, :, at].astype(F32) * spread[k * 64 : (k + 1) * 64]
+        return sum_ * factor
+
+    for n, q in enumerate((2, 1, 3)):
+        sum_ = increment(q)
+        for h in range(2):
+            sendy[q - 1, h] = sum_[:, h * 128 : (h + 1) * 128].astype(BF16)
+        if n == 0:
+            pl.semaphore_wait(barrier, len(greet))
+        go(("yr", q))
+    whole = increment(0)
     for load in loads[:LOADS]:
         load.wait()
-    turn(0, slots // 2)
     got(("yr", 1), ("yr", 3), ("yr", 2))
     for h in range(2):
-        whole = partial_ref[:, pl.ds(pl.multiple_of(e * 256 + h * 128, 128), 128)]
+        half = whole[:, h * 128 : (h + 1) * 128]
         for q in range(3):
-            whole = whole + recvy[q, h].astype(F32)
-        own[0][0][2 * e + h] = whole.astype(BF16)
-    go(("yg", 1), ("yg", 3), ("yg", 2))
-    turn(slots // 2, slots // 2)
+            half = half + recvy[q, h].astype(F32)
+        own[0][0][2 * e + h] = half.astype(BF16)
+    go(("yg", 2), ("yg", 1), ("yg", 3))
+    turn(0, slots // 2)
     got(("yg", 1), ("yg", 3), ("yg", 2))
-    go("A3", "A1", ("B", 3, 0), ("B", 1, 0), ("C", 0, 0))
+    go("A3", "A1", ("C", 0, 0))
+    turn(slots // 2, slots // 4)
+    go(("B", 3, 0), ("B", 1, 0))
+    turn(slots // 4 * 3, slots // 4)
+    lax.fori_loop(0, slots // 8, tables, 0)
     for load in loads[LOADS:]:
         load.wait()
     for f in range(2):
@@ -363,8 +426,20 @@
         copy_of(name).wait_send()
 
 
-def exchange(partial_sum, innovation, obs_precision, obs_weight, obs_vertical, meta):
-    levels, columns = partial_sum.shape
+def exchange(
+    factor,
+    block_column,
+    tile_count,
+    loc_vertical,
+    innovation,
+    obs_precision,
+    perturbations,
+    control,
+    loc_horizontal,
+    obs_weight,
+    obs_vertical,
+):
+    members, levels, columns = control.shape
     slots, block, _ = obs_weight.shape
     smem = pl.BlockSpec(memory_space=pltpu.SMEM)
     vmem = pl.BlockSpec(memory_space=pltpu.VMEM)
@@ -374,16 +449,22 @@
         return pltpu.VMEM((*lead, levels, block), dtype)
 
     return pl.pallas_call(
-        exchange_kernel,
+        functools.partial(exchange_kernel, factor),
         out_shape=jax.ShapeDtypeStruct((levels, columns), F32),
-        in_specs=[smem] * 4 + [vmem] * 3 + [hbm] * 2,
+        in_specs=[smem] * 2 + [vmem] * 3 + [hbm] * 5,
         out_specs=vmem,
         scratch_shapes=[blocks(8) for _ in range(32)]
         + [
+            pltpu.VMEM((members, levels, columns), BF16),
+            pltpu.VMEM((members, levels, columns), F32),
+            pltpu.VMEM((columns, columns), BF16),
+            pltpu.VMEM((members * levels, columns), BF16),
+            pltpu.SMEM((slots,), jnp.int32),
+            pltpu.SMEM((slots,), jnp.int32),
             pltpu.VMEM((slots, block, block), BF16),
             pltpu.VMEM((slots, block, block), BF16),
             pltpu.VMEM((slots, levels, block), F32),
-            blocks(8),
+            blocks(3, 2),
             blocks(3, 2),
             blocks(16),
             blocks(18, dtype=F32),
@@ -399,14 +480,25 @@
             blocks(8),
             blocks(3, 2),
             blocks(8),
-            pltpu.SemaphoreType.DMA((2 * LOADS,)),
+            pltpu.SemaphoreType.DMA((2 * LOADS + 3,)),
             pltpu.SemaphoreType.DMA((112,)),
             pltpu.SemaphoreType.DMA((112,)),
         ],
         compiler_params=pltpu.CompilerParams(
-            collective_id=0, has_side_effects=True, vmem_limit_bytes=52 * 1024 * 1024
+            collective_id=0, has_side_effects=True, vmem_limit_bytes=56 * 1024 * 1024
         ),
-    )(*meta, partial_sum, innovation, obs_precision, obs_weight, obs_vertical)
+    )(
+        block_column,
+        tile_count,
+        loc_vertical,
+        innovation,
+        obs_precision,
+        perturbations,
+        control,
+        loc_horizontal,
+        obs_weight,
+        obs_vertical,
+    )
 
 
 def on_device(
@@ -422,34 +514,20 @@
     tile_count,
 ):
     members_dev, levels, columns = control.shape
-    tile_total = lax.axis_size("tile")
     ens_total = lax.axis_size("ens")
     factor = 1.0 / math.sqrt(members_dev * ens_total - 1)
-    vertical = jnp.einsum(
-        "ml,klc->kmc", loc_vertical, control, precision=lax.Precision.HIGHEST
-    ).astype(BF16)
-    spread = jnp.dot(
-        vertical.reshape(members_dev * levels, columns),
-        loc_horizontal,
-        preferred_element_type=F32,
-    ).reshape(members_dev, levels, columns)
-    partial_sum = jnp.sum(perturbations.astype(F32) * spread, axis=0) * factor
-
-    slots = block_column.reshape(tile_total, 8)
-    place = jnp.arange(8, dtype=jnp.int32)
-    same = (slots[:, :, None] == slots[:, None, :]) & (place[:, None] > place[None, :])
-    prev = jnp.max(jnp.where(same, place[None, None, :], -1), axis=2)
-    prev = jnp.where(prev < 0, 8, prev).reshape(-1)
-    holds = slots[:, None, :] == place[None, :, None]
-    last = jnp.max(jnp.where(holds, place[None, None, :], -1), axis=2)
-    last = jnp.where(last < 0, 8, last).reshape(-1)
     adjoint = exchange(
-        partial_sum,
+        factor,
+        block_column,
+        tile_count,
+        loc_vertical,
         innovation,
         obs_precision,
+        perturbations,
+        control,
+        loc_horizontal,
         obs_weight,
         obs_vertical,
-        (block_column, tile_count, prev, last),
     )
     product_field = perturbations.astype(F32) * adjoint[None]
     back_vertical = jnp.einsum(

time: 72 us -> 71.9 us (level); the launches traced: 71.8 us -> 70.7 us
  Pallas kernels: 60.5 us -> 64.7 us
  matrix products: 9.7 us -> 5.93 us
  local copies, waits for them, and re-layouts: 1.35 us -> 0.02 us
    dot_general x2 -> x0, matrix products: 4.87 us -> none  [the longest x1 3.58 us: on_device(): jnp.einsum('ml,klc->kmc', loc_vertical, control, precision=lax.Precision....]
    pallas_call x1, Pallas kernels: 60.5 us -> 64.7 us  [exchange(): pl.pallas_call(functools.partial(exchange_kernel, factor), out_shape=jax....]
    dot_general x1, matrix products: 2.19 us -> 3.28 us  [on_device(): jnp.einsum('ml,kmc->klc', loc_vertical, product_field, precision=lax.Prec...]
    eq x2 -> x0, local copies, waits for them, and re-layouts: 0.98 us -> none  [on_device(): slots[:, :, None] == slots[:, None, :]]
where the time goes in v4:
time: 71.9 us; the launch traced here: 70.7 us
  Pallas kernels  64.7 us (90%)
  matrix products  5.93 us (8%)
    pallas_call x1, Pallas kernels, exchange(): pl.pallas_call(functools.partial(exchange_kernel, factor), out_shape=jax....  64.7 us
    dot_general x1, matrix products, on_device(): jnp.einsum('ml,kmc->klc', loc_vertical, product_field, precision=lax.Prec...  3.28 us
    dot_general x1, matrix products, on_device(): jnp.einsum('rc,dc->rd', back_vertical.reshape(members_dev * levels, colum...  2.65 us

profile of v4, /device:TPU:6, one launch (start us, length us, event | category | flops | bytes accessed | tf_op | source)
XLA Modules:
  0.0 70.7 jit_solution(9208929073364295265)
XLA Ops:
  0.0 0.0 copy-start.3
  0.0 0.0 copy-start
  0.0 0.0 copy-start.2
  0.0 64.7 %shard_map.100 = f32[64,1024]{1,0:T(8,128)} custom-call(s32[256]{0:T(256)} %block_ref.1, s32[32]{0:T(128)} %count_ref.1, f32[64,64]{1,0:T(8,128)} %loc_vertical_ref.1, f32[256,128]{1,0:T(8,128)} %innov_ref.1, f32[256,128]{1,0:T(8,128)} %prec_ref.1, bf16[8,64,1024]{2,1,0:T(8,128)(2,1)} %pert_hbm.1, f32[8,64,1024]{2,1,0:T(8,128)} %control_hbm.1, ...), custom_call_target="tpu_custom_call" | custom-call | tf_op jit(solution)/shard_map/pallas_call | solution.py:451
  64.7 0.0 copy-done.3
  64.7 0.0 copy-done
  64.7 0.0 copy-start.1
  64.7 3.3 %fusion.10 = bf16[8,64,1024]{2,1,0:T(8,128)(2,1)S(1)} fusion(bf16[8,64,1024]{2,1,0:T(8,128)(2,1)S(1)} %copy-done, f32[64,1024]{1,0:T(8,128)} %shard_map.100, f32[64,64]{1,0:T(8,128)S(1)} %copy-done.3), kind=kOutput, calls=%fused_computation.7 | convolution fusion | flops 404226048 | bytes 2375680 | tf_op jit(solution)/shard_map/ml,kmc->klc/dot_general | solution.py:533
  68.0 0.0 copy-done.2
  68.0 0.0 copy-done.1
  68.0 2.6 %multiply_add_fusion = f32[8,64,1024]{2,1,0:T(8,128)} fusion(f32[8,64,1024]{2,1,0:T(8,128)S(1)} %copy-done.1, bf16[8,64,1024]{2,1,0:T(8,128)(2,1)S(1)} %fusion.10, bf16[1024,1024]{1,0:T(8,128)(2,1)S(1)} %copy-done.2), kind=kOutput, calls=%fused_computation.2 | convolution fusion | flops 1074790400 | bytes 7340032 | tf_op jit(solution)/shard_map/rc,dc->rd/dot_general | solution.py:536
Async XLA Ops:
  0.0 64.7 %copy-start.3 = (f32[64,64]{1,0:T(8,128)S(1)}, f32[64,64]{1,0:T(8,128)}, u32[]{:S(2)}) copy-start(f32[64,64]{1,0:T(8,128)} %loc_vertical_ref.1) | copy-start | bytes 49156
  0.0 64.7 %copy-start = (bf16[8,64,1024]{2,1,0:T(8,128)(2,1)S(1)}, bf16[8,64,1024]{2,1,0:T(8,128)(2,1)}, u32[]{:S(2)}) copy-start(bf16[8,64,1024]{2,1,0:T(8,128)(2,1)} %pert_hbm.1) | copy-start | bytes 3145732
  0.0 68.0 %copy-start.2 = (bf16[1024,1024]{1,0:T(8,128)(2,1)S(1)}, bf16[1024,1024]{1,0:T(8,128)(2,1)}, u32[]{:S(2)}) copy-start(bf16[1024,1024]{1,0:T(8,128)(2,1)} %horizontal_hbm.1) | copy-start | bytes 6291460
  64.7 3.3 %copy-start.1 = (f32[8,64,1024]{2,1,0:T(8,128)S(1)}, f32[8,64,1024]{2,1,0:T(8,128)}, u32[]{:S(2)}) copy-start(f32[8,64,1024]{2,1,0:T(8,128)} %control_hbm.1) | copy-start | bytes 6291460

commit v5 on v4

--- a/solution.py
+++ b/solution.py
@@ -65,7 +65,6 @@
         prev_ref,
         last_ref,
         weight,
-        turned,
         vertical,
         sendy,
         recvy,
@@ -190,14 +189,6 @@
         way(("ur", q), unit_b.at[pl.ds(2 * ((e + q) % SIDE), 2)], unit_in.at[q - 1], y_dev[q])
         way(("ug", q), done, done, y_dev[q])
 
-    def turn(first, count):
-        def some(i, carry):
-            for u in range(4):
-                turned[i * 4 + u] = weight[i * 4 + u].T
-            return carry
-
-        lax.fori_loop(first // 4, (first + count) // 4, some, 0)
-
     def tables(j, carry):
         base = j * 8
         columns = [block_ref[base + p] for p in range(8)]
@@ -247,8 +238,6 @@
             pl.semaphore_wait(barrier, len(greet))
         go(("yr", q))
     whole = increment(0)
-    for load in loads[:LOADS]:
-        load.wait()
     got(("yr", 1), ("yr", 3), ("yr", 2))
     for h in range(2):
         half = whole[:, h * 128 : (h + 1) * 128]
@@ -256,14 +245,11 @@
             half = half + recvy[q, h].astype(F32)
         own[0][0][2 * e + h] = half.astype(BF16)
     go(("yg", 2), ("yg", 1), ("yg", 3))
-    turn(0, slots // 2)
+    lax.fori_loop(0, slots // 8, tables, 0)
     got(("yg", 1), ("yg", 3), ("yg", 2))
     go("A3", "A1", ("C", 0, 0))
-    turn(slots // 2, slots // 4)
     go(("B", 3, 0), ("B", 1, 0))
-    turn(slots // 4 * 3, slots // 4)
-    lax.fori_loop(0, slots // 8, tables, 0)
-    for load in loads[LOADS:]:
+    for load in loads:
         load.wait()
     for f in range(2):
         chain[f * 9 + 8] = jnp.zeros((64, 128), F32)
@@ -345,7 +331,12 @@
         innov = [innov_ref[pl.ds(base, 8), :] for _, _, base in pairs]
         prec = [prec_ref[pl.ds(base, 8), :] for _, _, base in pairs]
         projs = [
-            jnp.dot(picked[f * 8 + p], turned[base + p], preferred_element_type=F32)
+            lax.dot_general(
+                picked[f * 8 + p],
+                weight[base + p],
+                (((1,), (1,)), ((), ())),
+                preferred_element_type=F32,
+            )
             for f, tile, base, p in both
         ]
         deps = []
@@ -419,9 +410,24 @@
             sum_ = sum_ + unit_in[q, h].astype(F32)
         final[2 * e + h] = sum_.astype(BF16)
     go(("ug", 1), ("ug", 3), ("ug", 2))
-    got(("ug", 1), ("ug", 3), ("ug", 2))
-    for k in range(8):
-        out_ref[:, k * 128 : (k + 1) * 128] = final[k].astype(F32)
+    lv_t = loc_vertical_ref[...].T
+    head_t = lv_t.astype(BF16)
+    heads_t = jnp.concatenate([head_t, (lv_t - head_t.astype(F32)).astype(BF16)], axis=0)
+    for q in (0, 1, 3, 2):
+        if q > 0:
+            got(("ug", (4 - q)))
+        chunk_at = (e + q) % SIDE
+        at = pl.ds(pl.multiple_of(chunk_at * 256, 256), 256)
+        adjoint = jnp.concatenate(
+            [final[2 * chunk_at].astype(F32), final[2 * chunk_at + 1].astype(F32)], axis=1
+        )
+        for k in range(8):
+            field = pert[k, :, at].astype(F32) * adjoint
+            field_head = field.astype(BF16)
+            field_rest = (field - field_head.astype(F32)).astype(BF16)
+            two = jnp.dot(heads_t, field_head, preferred_element_type=F32)
+            sum_ = two[:64] + two[64:] + jnp.dot(head_t, field_rest, preferred_element_type=F32)
+            out_ref[k * 64 : (k + 1) * 64, at] = sum_.astype(BF16)
     for name in ways:
         copy_of(name).wait_send()
 
@@ -450,7 +456,7 @@
 
     return pl.pallas_call(
         functools.partial(exchange_kernel, factor),
-        out_shape=jax.ShapeDtypeStruct((levels, columns), F32),
+        out_shape=jax.ShapeDtypeStruct((members * levels, columns), BF16),
         in_specs=[smem] * 2 + [vmem] * 3 + [hbm] * 5,
         out_specs=vmem,
         scratch_shapes=[blocks(8) for _ in range(32)]
@@ -461,7 +467,6 @@
             pltpu.VMEM((members * levels, columns), BF16),
             pltpu.SMEM((slots,), jnp.int32),
             pltpu.SMEM((slots,), jnp.int32),
-            pltpu.VMEM((slots, block, block), BF16),
             pltpu.VMEM((slots, block, block), BF16),
             pltpu.VMEM((slots, levels, block), F32),
             blocks(3, 2),
@@ -516,7 +521,7 @@
     members_dev, levels, columns = control.shape
     ens_total = lax.axis_size("ens")
     factor = 1.0 / math.sqrt(members_dev * ens_total - 1)
-    adjoint = exchange(
+    back_vertical = exchange(
         factor,
         block_column,
         tile_count,
@@ -529,13 +534,9 @@
         obs_weight,
         obs_vertical,
     )
-    product_field = perturbations.astype(F32) * adjoint[None]
-    back_vertical = jnp.einsum(
-        "ml,kmc->klc", loc_vertical, product_field, precision=lax.Precision.HIGHEST
-    ).astype(BF16)
     spread_back = jnp.einsum(
         "rc,dc->rd",
-        back_vertical.reshape(members_dev * levels, columns),
+        back_vertical,
         loc_horizontal,
         preferred_element_type=F32,
     )

time: 71.9 us -> 69.7 us (0.969); the launches traced: 70.7 us -> 69.5 us
  matrix products: 5.93 us -> 2.66 us
  other arithmetic: 0 us -> 1.71 us
    dot_general x2 -> x1, matrix products: 5.93 us -> 2.66 us  [on_device(): jnp.einsum('rc,dc->rd', back_vertical, loc_horizontal, preferred_element_...]
    add x0 -> x1, other arithmetic: none -> 1.71 us  [on_device(): return control + factor * spread_back.reshape(members_dev, levels, columns)]
where the time goes in v5:
time: 69.7 us; the launch traced here: 69.5 us
  Pallas kernels  65.1 us (93%)
  matrix products  2.66 us (4%)
  other arithmetic  1.71 us (2%)
    pallas_call x1, Pallas kernels, exchange(): pl.pallas_call(functools.partial(exchange_kernel, factor), out_shape=jax....  65.1 us
    dot_general x1, matrix products, on_device(): jnp.einsum('rc,dc->rd', back_vertical, loc_horizontal, preferred_element_...  2.66 us
    add x1, other arithmetic, on_device(): return control + factor * spread_back.reshape(members_dev, levels, columns)  1.71 us

profile of v5, /device:TPU:6, one launch (start us, length us, event | category | flops | bytes accessed | tf_op | source)
XLA Modules:
  0.0 69.5 jit_solution(15879132903029235113)
XLA Ops:
  0.0 0.0 copy-start.1
  0.0 65.1 %shard_map.100 = bf16[512,1024]{1,0:T(8,128)(2,1)} custom-call(s32[256]{0:T(256)} %block_ref.1, s32[32]{0:T(128)} %count_ref.1, f32[64,64]{1,0:T(8,128)} %loc_vertical_ref.1, f32[256,128]{1,0:T(8,128)} %innov_ref.1, f32[256,128]{1,0:T(8,128)} %prec_ref.1, bf16[8,64,1024]{2,1,0:T(8,128)(2,1)} %pert_hbm.1, f32[8,64,1024]{2,1,0:T(8,128)} %control_hbm.1, ...), custom_call_target="tpu_custom_call" | custom-call | tf_op jit(solution)/shard_map/pallas_call | solution.py:457
  65.1 0.0 copy-done.1
  65.1 0.0 copy-start
  65.2 2.7 %convolution_multiply_fusion = f32[512,1024]{1,0:T(8,128)S(1)} fusion(bf16[512,1024]{1,0:T(8,128)(2,1)} %shard_map.100, bf16[1024,1024]{1,0:T(8,128)(2,1)S(1)} %copy-done.1), kind=kOutput, calls=%fused_computation | convolution fusion | flops 1074266112 | bytes 5242880 | tf_op jit(solution)/shard_map/rc,dc->rd/dot_general | solution.py:537
  67.8 0.0 copy-done
  67.8 1.7 %add.3 = f32[8,64,1024]{2,1,0:T(8,128)} add(f32[8,64,1024]{2,1,0:T(8,128)S(1)} %copy-done, f32[8,64,1024]{2,1,0:T(8,128)S(1)} %bitcast.3) | non-fusion elementwise | flops 524288 | bytes 6291456 | tf_op jit(solution)/shard_map/add | solution.py:543
Async XLA Ops:
  0.0 65.1 %copy-start.1 = (bf16[1024,1024]{1,0:T(8,128)(2,1)S(1)}, bf16[1024,1024]{1,0:T(8,128)(2,1)}, u32[]{:S(2)}) copy-start(bf16[1024,1024]{1,0:T(8,128)(2,1)} %horizontal_hbm.1) | copy-start | bytes 6291460
  65.1 2.7 %copy-start = (f32[8,64,1024]{2,1,0:T(8,128)S(1)}, f32[8,64,1024]{2,1,0:T(8,128)}, u32[]{:S(2)}) copy-start(f32[8,64,1024]{2,1,0:T(8,128)} %control_hbm.1) | copy-start | bytes 6291460

commit v6 on v5

--- a/solution.py
+++ b/solution.py
@@ -24,15 +24,19 @@
     (3, 3), (1, 3), (3, 2), (1, 2), (2, 0), (2, 1), (2, 3), (2, 2),
 )
 ARRIVE = {
-    1: ((0, 3), (0, 1), (3, 0), (1, 0)),
-    3: ((0, 2),),
-    5: ((3, 1), (1, 1)),
-    7: ((3, 3), (1, 3)),
-    9: ((3, 2), (1, 2)),
-    11: ((2, 0),),
-    12: ((2, 1),),
-    13: ((2, 3),),
-    14: ((2, 2),),
+    1: (
+        (0, 0, 3), (0, 0, 1), (1, 0, 3), (1, 0, 1),
+        (0, 3, 0), (0, 1, 0), (1, 3, 0), (1, 1, 0),
+    ),
+    3: ((1, 0, 2),),
+    5: ((0, 3, 3), (0, 1, 1), (0, 3, 1), (0, 1, 3), (1, 3, 1), (1, 1, 1)),
+    7: ((1, 3, 3), (1, 1, 3)),
+    8: ((0, 3, 2), (0, 1, 2)),
+    9: ((1, 3, 2), (1, 1, 2)),
+    10: ((1, 2, 0),),
+    12: ((1, 2, 1),),
+    13: ((1, 2, 3),),
+    14: ((1, 2, 2),),
 }
 STEP_OF = {place: i for i, place in enumerate(ORDER)}
 STEPS = len(ORDER)
@@ -65,6 +69,7 @@
         prev_ref,
         last_ref,
         weight,
+        turned,
         vertical,
         sendy,
         recvy,
@@ -159,13 +164,15 @@
     for q in (1, 2, 3):
         way(("yr", q), sendy.at[q - 1], recvy.at[q - 1], y_dev[q])
         way(("yg", q), mine, mine, y_dev[q])
-    way("A3", own[0][0], own[0][3], lo_dev[1])
-    way("A1", own[0][0], own[0][1], lo_dev[3])
+    for part, at in (("l", low), ("h", high)):
+        way(("A", 3, part), own[0][0].at[at], own[0][3].at[at], lo_dev[1])
+        way(("A", 1, part), own[0][0].at[at], own[0][1].at[at], lo_dev[3])
     way("A2a", own[0][3].at[low], own[0][2].at[low], lo_dev[1])
     way("A2b", own[0][1].at[high], own[0][2].at[high], lo_dev[3])
     for rho in range(4):
-        way(("B", 3, rho), own[0][rho], own[3][rho], hi_dev[1])
-        way(("B", 1, rho), own[0][rho], own[1][rho], hi_dev[3])
+        for part, at in (("l", low), ("h", high)):
+            way(("B", 3, rho, part), own[0][rho].at[at], own[3][rho].at[at], hi_dev[1])
+            way(("B", 1, rho, part), own[0][rho].at[at], own[1][rho].at[at], hi_dev[3])
         way(("F", 0, rho), own[3][rho].at[low], own[2][rho].at[low], hi_dev[1])
         way(("F", 1, rho), own[1][rho].at[high], own[2][rho].at[high], hi_dev[3])
         for r in range(4):
@@ -182,12 +189,23 @@
         way(("R0a", rho), total_at(1, rho, 0, 4), row_in.at[pl.ds(rho * 8, 4)], hi_dev[1])
         way(("R1u", rho), total_at(3, rho, 0, 4), row_in.at[pl.ds(32 + rho * 8, 4)], hi_dev[3])
         way(("R1a", rho), total_at(3, rho, 4, 4), row_in.at[pl.ds(32 + rho * 8 + 4, 4)], hi_dev[3])
-    for rho in (1, 2, 3):
+    for q in range(4):
+        at = 2 * ((e + q) % SIDE)
+        way(("L2", q), plane.at[pl.ds(16 + at, 2)], plane_in.at[pl.ds(8 + at, 2)], lo_dev[2])
+    for rho in (1, 3):
         way(("L", rho), plane.at[pl.ds(rho * 8, 8)], plane_in.at[pl.ds((rho - 1) * 8, 8)], lo_dev[rho])
     done = final.at[pl.ds(2 * e, 2)]
     for q in (1, 2, 3):
         way(("ur", q), unit_b.at[pl.ds(2 * ((e + q) % SIDE), 2)], unit_in.at[q - 1], y_dev[q])
         way(("ug", q), done, done, y_dev[q])
+
+    def turn(first, count):
+        def some(i, carry):
+            for u in range(8):
+                turned[i * 8 + u] = weight[i * 8 + u].T
+            return carry
+
+        lax.fori_loop(first // 8, (first + count) // 8, some, 0)
 
     def tables(j, carry):
         base = j * 8
@@ -246,32 +264,51 @@
         own[0][0][2 * e + h] = half.astype(BF16)
     go(("yg", 2), ("yg", 1), ("yg", 3))
     lax.fori_loop(0, slots // 8, tables, 0)
+    for load in loads[:LOADS]:
+        load.wait()
+    turn(0, slots // 2)
     got(("yg", 1), ("yg", 3), ("yg", 2))
-    go("A3", "A1", ("C", 0, 0))
-    go(("B", 3, 0), ("B", 1, 0))
-    for load in loads:
+    go(("A", 3, "l"), ("A", 1, "h"), ("A", 3, "h"), ("A", 1, "l"))
+    go(("B", 3, 0, "l"), ("B", 1, 0, "h"), ("C", 0, 0), ("B", 3, 0, "h"), ("B", 1, 0, "l"))
+    turn(slots // 2, slots // 2)
+    for load in loads[LOADS:]:
         load.wait()
     for f in range(2):
         chain[f * 9 + 8] = jnp.zeros((64, 128), F32)
 
-    def arrived(r, rho):
+    def forward(r, rho):
+        if r == 0:
+            if rho == 3:
+                got(("A", 3, "l"))
+                go("A2a", ("B", 3, 3, "l"))
+            else:
+                got(("A", 1, "h"))
+                go("A2b", ("B", 1, 1, "h"))
+        else:
+            got(("B", r, rho, "l" if r == 3 else "h"))
+            go(("F", 0 if r == 3 else 1, rho))
+
+    def complete(r, rho):
         if r == 0 and rho == 2:
-            got("A2a", "A2b")
+            got("A2a")
+            go(("B", 3, 2, "l"))
+            got("A2b")
+            go(("B", 1, 2, "h"), ("B", 1, 2, "l"), ("B", 3, 2, "h"))
+        elif r == 0 and rho == 3:
+            got(("A", 3, "h"))
+            go(("B", 1, 3, "h"), ("B", 3, 3, "h"), ("B", 1, 3, "l"))
         elif r == 0:
-            got("A%d" % rho)
-            go("A2a" if rho == 3 else "A2b")
+            got(("A", 1, "l"))
+            go(("B", 3, 1, "l"), ("B", 1, 1, "l"), ("B", 3, 1, "h"))
         elif r == 2:
             got(("F", 0, rho), ("F", 1, rho))
         else:
-            got(("B", r, rho))
-            go(("F", 0 if r == 3 else 1, rho))
-        if r == 0:
-            go(("B", 3, rho), ("B", 1, rho))
+            got(("B", r, rho, "h" if r == 3 else "l"))
         go(("C", r, rho))
 
     def event(i):
-        for place in ARRIVE.get(i, ()):
-            arrived(*place)
+        for whole_tile, r, rho in ARRIVE.get(i, ()):
+            (complete if whole_tile else forward)(r, rho)
         if i == 13:
             for rho in LATE:
                 go(("R0u", rho), ("R1u", rho))
@@ -331,12 +368,7 @@
         innov = [innov_ref[pl.ds(base, 8), :] for _, _, base in pairs]
         prec = [prec_ref[pl.ds(base, 8), :] for _, _, base in pairs]
         projs = [
-            lax.dot_general(
-                picked[f * 8 + p],
-                weight[base + p],
-                (((1,), (1,)), ((), ())),
-                preferred_element_type=F32,
-            )
+            jnp.dot(picked[f * 8 + p], turned[base + p], preferred_element_type=F32)
             for f, tile, base, p in both
         ]
         deps = []
@@ -392,20 +424,29 @@
                 unit[k] = sum_
             else:
                 plane[rho * 8 + k] = sum_.astype(BF16)
-        if rho != 0:
+        if rho == 2:
+            go(*[("L2", q) for q in (2, 1, 3, 0)])
+        elif rho != 0:
             go(("L", rho))
-    got(("L", 1), ("L", 3), ("L", 2))
-    for k in range(8):
-        sum_ = unit[k]
-        for q in range(3):
-            sum_ = sum_ + plane_in[q * 8 + k].astype(F32)
-        unit[k] = sum_
-        unit_b[k] = sum_.astype(BF16)
-
-    go(("ur", 1), ("ur", 3), ("ur", 2))
+    got(("L", 1), ("L", 3))
+
+    kept = []
+    for q in (2, 1, 3, 0):
+        got(("L2", q))
+        for h in range(2):
+            k = 2 * ((e + q) % SIDE) + h
+            sum_ = unit[k]
+            for n in range(3):
+                sum_ = sum_ + plane_in[n * 8 + k].astype(F32)
+            if q == 0:
+                kept.append(sum_)
+            else:
+                unit_b[k] = sum_.astype(BF16)
+        if q != 0:
+            go(("ur", q))
     got(("ur", 1), ("ur", 3), ("ur", 2))
     for h in range(2):
-        sum_ = unit[2 * e + h]
+        sum_ = kept[h]
         for q in range(3):
             sum_ = sum_ + unit_in[q, h].astype(F32)
         final[2 * e + h] = sum_.astype(BF16)
@@ -468,6 +509,7 @@
             pltpu.SMEM((slots,), jnp.int32),
             pltpu.SMEM((slots,), jnp.int32),
             pltpu.VMEM((slots, block, block), BF16),
+            pltpu.VMEM((slots, block, block), BF16),
             pltpu.VMEM((slots, levels, block), F32),
             blocks(3, 2),
             blocks(3, 2),
@@ -486,8 +528,8 @@
             blocks(3, 2),
             blocks(8),
             pltpu.SemaphoreType.DMA((2 * LOADS + 3,)),
-            pltpu.SemaphoreType.DMA((112,)),
-            pltpu.SemaphoreType.DMA((112,)),
+            pltpu.SemaphoreType.DMA((128,)),
+            pltpu.SemaphoreType.DMA((128,)),
         ],
         compiler_params=pltpu.CompilerParams(
             collective_id=0, has_side_effects=True, vmem_limit_bytes=56 * 1024 * 1024
@@ -535,12 +577,10 @@
         obs_vertical,
     )
     spread_back = jnp.einsum(
-        "rc,dc->rd",
-        back_vertical,
-        loc_horizontal,
-        preferred_element_type=F32,
+        "rc,dc->rd", back_vertical, loc_horizontal, preferred_element_type=F32
     )
-    return control + factor * spread_back.reshape(members_dev, levels, columns)
+    flat_control = control.reshape(members_dev * levels, columns)
+    return (flat_control + factor * spread_back).reshape(control.shape)
 
 
 def solution(mesh):

time: 69.7 us -> 68.7 us (0.986)
  other arithmetic: 1.71 us -> 0 us
  matrix products: 2.66 us -> 3.84 us
    add x1 -> x0, other arithmetic: 1.71 us -> none  [on_device(): return control + factor * spread_back.reshape(members_dev, levels, columns)]
    dot_general x1, matrix products: 2.66 us -> 3.84 us  [on_device(): jnp.einsum('rc,dc->rd', back_vertical, loc_horizontal, preferred_element_...]
where the time goes in v6:
time: 68.7 us; the launch traced here: 68.6 us
  Pallas kernels  64.7 us (94%)
  matrix products  3.84 us (6%)
    pallas_call x1, Pallas kernels, exchange(): pl.pallas_call(functools.partial(exchange_kernel, factor), out_shape=jax....  64.7 us
    dot_general x1, matrix products, on_device(): jnp.einsum('rc,dc->rd', back_vertical, loc_horizontal, preferred_element_...  3.84 us

profile of v6, /device:TPU:6, one launch (start us, length us, event | category | flops | bytes accessed | tf_op | source)
XLA Modules:
  0.0 68.6 jit_solution(13055022227618777163)
XLA Ops:
  0.0 0.0 copy-start.1
  0.0 0.0 copy-start
  0.0 64.7 %shard_map.100 = bf16[512,1024]{1,0:T(8,128)(2,1)} custom-call(s32[256]{0:T(256)} %block_ref.1, s32[32]{0:T(128)} %count_ref.1, f32[64,64]{1,0:T(8,128)} %loc_vertical_ref.1, f32[256,128]{1,0:T(8,128)} %innov_ref.1, f32[256,128]{1,0:T(8,128)} %prec_ref.1, bf16[8,64,1024]{2,1,0:T(8,128)(2,1)} %pert_hbm.1, f32[8,64,1024]{2,1,0:T(8,128)} %control_hbm.1, ...), custom_call_target="tpu_custom_call" | custom-call | tf_op jit(solution)/shard_map/pallas_call | solution.py:498
  64.7 0.0 copy-done.1
  64.7 0.0 copy-done
  64.7 3.8 %bitcast_add_fusion = f32[512,1024]{1,0:T(8,128)} fusion(f32[8,64,1024]{2,1,0:T(8,128)S(1)} %copy-done, bf16[512,1024]{1,0:T(8,128)(2,1)} %shard_map.100, bf16[1024,1024]{1,0:T(8,128)(2,1)S(1)} %copy-done.1), kind=kOutput, calls=%fused_computation | convolution fusion | flops 1074790400 | bytes 7340032 | tf_op jit(solution)/shard_map/rc,dc->rd/dot_general | solution.py:579
Async XLA Ops:
  0.0 64.7 %copy-start.1 = (bf16[1024,1024]{1,0:T(8,128)(2,1)S(1)}, bf16[1024,1024]{1,0:T(8,128)(2,1)}, u32[]{:S(2)}) copy-start(bf16[1024,1024]{1,0:T(8,128)(2,1)} %horizontal_hbm.1) | copy-start | bytes 6291460
  0.0 64.7 %copy-start = (f32[8,64,1024]{2,1,0:T(8,128)S(1)}, f32[8,64,1024]{2,1,0:T(8,128)}, u32[]{:S(2)}) copy-start(f32[8,64,1024]{2,1,0:T(8,128)} %control_hbm.1) | copy-start | bytes 6291460

commit v7 on v6

--- a/solution.py
+++ b/solution.py
@@ -40,6 +40,7 @@
 }
 STEP_OF = {place: i for i, place in enumerate(ORDER)}
 STEPS = len(ORDER)
+STRAIGHT = STEPS - 2
 LATE = (0, 1, 3, 2)
 
 
@@ -80,6 +81,7 @@
         core_in,
         total,
         half_in,
+        half_other,
         row_in,
         plane,
         plane_in,
@@ -112,7 +114,6 @@
         for i in range(LOADS):
             at = pl.ds(i * chunk, chunk)
             copy = pltpu.make_async_copy(src.at[at], dst.at[at], load_sem.at[n * LOADS + i])
-            copy.start()
             loads.append(copy)
 
     def beside(zq, xq):
@@ -122,6 +123,9 @@
     hi_dev = {q: (e, jnp.where(c == 0, beside(q, 0), beside(0, q))) for q in (1, 3)}
     lo_dev = {q: (e, jnp.where(c == 0, beside(0, q), beside(q, 0))) for q in (1, 2, 3)}
     core_dev = (e, tile_of(z, x, 1 - c))
+    swap = 1 - 2 * c
+    hi_cross = {q: (e, hi_dev[q][1] + swap) for q in (1, 3)}
+    lo_cross = {q: (e, lo_dev[q][1] + swap) for q in (1, 3)}
 
     def slot_tile(core, r, rho):
         hi = (jnp.where(core == 0, z, x) + r) % SIDE
@@ -130,6 +134,7 @@
 
     barrier = pltpu.get_barrier_semaphore()
     greet = [*y_dev.values(), *hi_dev.values(), *lo_dev.values(), core_dev]
+    greet += [*hi_cross.values(), *lo_cross.values()]
     for dev in greet:
         pl.semaphore_signal(barrier, inc=1, device_id=dev, device_id_type=MESH)
     ways = {}
@@ -157,7 +162,7 @@
             copy_of(name).wait_recv()
 
     low, high = pl.ds(0, 4), pl.ds(4, 4)
-    for i, (r, rho) in enumerate(ORDER):
+    for i in range(STRAIGHT):
         at = pl.ds(i * 8, 8)
         way(("D", i), adj_other.at[at], core_in.at[at], core_dev)
     mine = own[0][0].at[pl.ds(2 * e, 2)]
@@ -176,15 +181,25 @@
         way(("F", 0, rho), own[3][rho].at[low], own[2][rho].at[low], hi_dev[1])
         way(("F", 1, rho), own[1][rho].at[high], own[2][rho].at[high], hi_dev[3])
         for r in range(4):
-            way(("C", r, rho), own[r][rho], other[r][rho], core_dev)
+            if (r, rho) != (2, 2):
+                way(("C", r, rho), own[r][rho], other[r][rho], core_dev)
 
     def total_at(r, rho, first, count):
         return total.at[pl.ds(STEP_OF[r, rho] * 8 + first, count)]
 
+    way(("FC", 0), own[3][2].at[low], other[2][2].at[low], hi_cross[1])
+    way(("FC", 1), own[1][2].at[high], other[2][2].at[high], hi_cross[3])
+    for i in range(STRAIGHT, STEPS):
+        for d, q in ((0, 1), (1, 3)):
+            src = adj_other.at[pl.ds(i * 8 + d * 4, 4)]
+            dst = half_other.at[pl.ds((i - STRAIGHT) * 8 + d * 4, 4)]
+            way(("HD", d, i), src, dst, lo_cross[q])
     for rho in range(4):
-        to_next, to_back = row_in.at[pl.ds(rho * 8, 8)], row_in.at[pl.ds(32 + rho * 8, 8)]
-        way(("H", 0, rho), total_at(2, rho, 0, 4), half_in.at[pl.ds(rho * 4, 4)], hi_dev[1])
-        way(("H", 1, rho), total_at(2, rho, 4, 4), half_in.at[pl.ds(16 + rho * 4, 4)], hi_dev[3])
+        i = STEP_OF[2, rho]
+        src = total if i < STRAIGHT else adj_own
+        for d, q in ((0, 1), (1, 3)):
+            dst = half_in.at[pl.ds(d * 16 + rho * 4, 4)]
+            way(("H", d, rho), src.at[pl.ds(i * 8 + d * 4, 4)], dst, hi_dev[q])
         way(("R0u", rho), total_at(1, rho, 4, 4), row_in.at[pl.ds(rho * 8 + 4, 4)], hi_dev[1])
         way(("R0a", rho), total_at(1, rho, 0, 4), row_in.at[pl.ds(rho * 8, 4)], hi_dev[1])
         way(("R1u", rho), total_at(3, rho, 0, 4), row_in.at[pl.ds(32 + rho * 8, 4)], hi_dev[3])
@@ -239,6 +254,8 @@
     lax.fori_loop(0, 8, one_member, 0)
     for load in first_loads[1:]:
         load.wait()
+    for load in loads:
+        load.start()
 
     def increment(q):
         at = pl.ds(pl.multiple_of((e + q) % SIDE * 256, 256), 256)
@@ -286,7 +303,10 @@
                 go("A2b", ("B", 1, 1, "h"))
         else:
             got(("B", r, rho, "l" if r == 3 else "h"))
-            go(("F", 0 if r == 3 else 1, rho))
+            d = 0 if r == 3 else 1
+            go(("F", d, rho))
+            if rho == 2:
+                go(("FC", d))
 
     def complete(r, rho):
         if r == 0 and rho == 2:
@@ -304,20 +324,24 @@
             got(("F", 0, rho), ("F", 1, rho))
         else:
             got(("B", r, rho, "h" if r == 3 else "l"))
-        go(("C", r, rho))
+        if (r, rho) != (2, 2):
+            go(("C", r, rho))
 
     def event(i):
-        for whole_tile, r, rho in ARRIVE.get(i, ()):
-            (complete if whole_tile else forward)(r, rho)
         if i == 13:
             for rho in LATE:
                 go(("R0u", rho), ("R1u", rho))
-        if i >= 2 and ORDER[i - 2][0] == 2:
+        if i - 2 in range(STEP_OF[2, 0], STRAIGHT):
             rho = ORDER[i - 2][1]
             go(("H", 0, rho), ("H", 1, rho))
+        for whole_tile, r, rho in ARRIVE.get(i, ()):
+            (complete if whole_tile else forward)(r, rho)
         if i < STEPS:
             r, rho = ORDER[i]
-            got(("C", r, rho))
+            if (r, rho) == (2, 2):
+                got(("FC", 0), ("FC", 1))
+            else:
+                got(("C", r, rho))
             for f, refs in ((0, own), (1, other)):
                 base = slot_tile(c if f == 0 else 1 - c, r, rho) * 8
                 for p in range(8):
@@ -337,15 +361,18 @@
         def _():
             dispatch(i, middle, last)
 
-    def add_core(i):
-        pltpu.make_async_remote_copy(
+    def core_copy(i):
+        return pltpu.make_async_remote_copy(
             src_ref=adj_other.at[pl.ds(i * 8, 8)],
             dst_ref=core_in.at[pl.ds(i * 8, 8)],
             send_sem=ssem.at[i],
             recv_sem=rsem.at[i],
             device_id=core_dev,
             device_id_type=MESH,
-        ).wait_recv()
+        )
+
+    def add_core(i):
+        core_copy(i).wait_recv()
         for k in range(8):
             both = adj_own[i * 8 + k].astype(F32) + core_in[i * 8 + k].astype(F32)
             total[i * 8 + k] = both.astype(BF16)
@@ -389,27 +416,33 @@
             into = adj_own if f == 0 else adj_other
             for k in range(8):
                 into[i * 8 + k] = chain[f * 9 + last_ref[base + k]].astype(BF16)
-        pltpu.make_async_remote_copy(
-            src_ref=adj_other.at[pl.ds(i * 8, 8)],
-            dst_ref=core_in.at[pl.ds(i * 8, 8)],
-            send_sem=ssem.at[i],
-            recv_sem=rsem.at[i],
-            device_id=core_dev,
-            device_id_type=MESH,
-        ).start()
+
+        @pl.when(i < STRAIGHT)
+        def _():
+            core_copy(i).start()
+
+        for last in range(STRAIGHT, STEPS):
+
+            @pl.when(i == last)
+            def _():
+                for d in range(2):
+                    go(("H", d, ORDER[last][1]), ("HD", d, last))
+
         return carry
 
     lax.fori_loop(0, STEPS, step, 0)
 
-    for i in (STEPS, STEPS + 1):
-        add_core(i - 2)
-        event(i)
     for rho in LATE:
         for d, r, first, name in ((0, 1, 0, "R0a"), (1, 3, 4, "R1a")):
             got(("H", d, rho))
+            straight = STEP_OF[2, rho] - STRAIGHT
+            if straight >= 0:
+                got(("HD", d, STEP_OF[2, rho]))
             for b in range(4):
                 at = STEP_OF[r, rho] * 8 + first + b
                 sum_ = total[at].astype(F32) + half_in[d * 16 + rho * 4 + b].astype(F32)
+                if straight >= 0:
+                    sum_ = sum_ + half_other[straight * 8 + d * 4 + b].astype(F32)
                 total[at] = sum_.astype(BF16)
             go((name, rho))
     for rho in (1, 3, 2, 0):
@@ -520,6 +553,7 @@
             blocks(128),
             blocks(128),
             blocks(32),
+            blocks(16),
             blocks(64),
             blocks(32),
             blocks(24),

time: 68.7 us -> 70.9 us (1.032)
  Pallas kernels: 64.7 us -> 66.9 us
    pallas_call x1, Pallas kernels: 64.7 us -> 66.9 us  [exchange(): pl.pallas_call(functools.partial(exchange_kernel, factor), out_shape=jax....]
where the time goes in v7:
time: 70.9 us; the launch traced here: 70.8 us
  Pallas kernels  66.9 us (94%)
  matrix products  3.84 us (5%)
    pallas_call x1, Pallas kernels, exchange(): pl.pallas_call(functools.partial(exchange_kernel, factor), out_shape=jax....  66.9 us
    dot_general x1, matrix products, on_device(): jnp.einsum('rc,dc->rd', back_vertical, loc_horizontal, preferred_element_...  3.84 us

profile of v7, /device:TPU:6, one launch (start us, length us, event | category | flops | bytes accessed | tf_op | source)
XLA Modules:
  0.0 70.8 jit_solution(15504960685775468141)
XLA Ops:
  0.0 0.0 copy-start.1
  0.0 0.0 copy-start
  0.0 66.9 %shard_map.100 = bf16[512,1024]{1,0:T(8,128)(2,1)} custom-call(s32[256]{0:T(256)} %block_ref.1, s32[32]{0:T(128)} %count_ref.1, f32[64,64]{1,0:T(8,128)} %loc_vertical_ref.1, f32[256,128]{1,0:T(8,128)} %innov_ref.1, f32[256,128]{1,0:T(8,128)} %prec_ref.1, bf16[8,64,1024]{2,1,0:T(8,128)(2,1)} %pert_hbm.1, f32[8,64,1024]{2,1,0:T(8,128)} %control_hbm.1, ...), custom_call_target="tpu_custom_call" | custom-call | tf_op jit(solution)/shard_map/pallas_call | solution.py:531
  66.9 0.0 copy-done.1
  66.9 0.0 copy-done
  66.9 3.8 %bitcast_add_fusion = f32[512,1024]{1,0:T(8,128)} fusion(f32[8,64,1024]{2,1,0:T(8,128)S(1)} %copy-done, bf16[512,1024]{1,0:T(8,128)(2,1)} %shard_map.100, bf16[1024,1024]{1,0:T(8,128)(2,1)S(1)} %copy-done.1), kind=kOutput, calls=%fused_computation | convolution fusion | flops 1074790400 | bytes 7340032 | tf_op jit(solution)/shard_map/rc,dc->rd/dot_general | solution.py:613
Async XLA Ops:
  0.0 66.9 %copy-start.1 = (bf16[1024,1024]{1,0:T(8,128)(2,1)S(1)}, bf16[1024,1024]{1,0:T(8,128)(2,1)}, u32[]{:S(2)}) copy-start(bf16[1024,1024]{1,0:T(8,128)(2,1)} %horizontal_hbm.1) | copy-start | bytes 6291460
  0.0 66.9 %copy-start = (f32[8,64,1024]{2,1,0:T(8,128)S(1)}, f32[8,64,1024]{2,1,0:T(8,128)}, u32[]{:S(2)}) copy-start(f32[8,64,1024]{2,1,0:T(8,128)} %control_hbm.1) | copy-start | bytes 6291460

commit v8 on v6

--- a/solution.py
+++ b/solution.py
@@ -307,14 +307,13 @@
         go(("C", r, rho))
 
     def event(i):
-        for whole_tile, r, rho in ARRIVE.get(i, ()):
-            (complete if whole_tile else forward)(r, rho)
-        if i == 13:
-            for rho in LATE:
-                go(("R0u", rho), ("R1u", rho))
         if i >= 2 and ORDER[i - 2][0] == 2:
             rho = ORDER[i - 2][1]
             go(("H", 0, rho), ("H", 1, rho))
+        for whole_tile, r, rho in ARRIVE.get(i, ()):
+            (complete if whole_tile else forward)(r, rho)
+        if i >= 2 and ORDER[i - 2][0] in (1, 3):
+            go(("R0u" if ORDER[i - 2][0] == 1 else "R1u", ORDER[i - 2][1]))
         if i < STEPS:
             r, rho = ORDER[i]
             got(("C", r, rho))

time: 68.7 us -> 67 us (0.975)
  Pallas kernels: 64.7 us -> 62.7 us
    pallas_call x1, Pallas kernels: 64.7 us -> 62.7 us  [exchange(): pl.pallas_call(functools.partial(exchange_kernel, factor), out_shape=jax....]
where the time goes in v8:
time: 67 us; the launch traced here: 66.5 us
  Pallas kernels  62.7 us (94%)
  matrix products  3.84 us (6%)
    pallas_call x1, Pallas kernels, exchange(): pl.pallas_call(functools.partial(exchange_kernel, factor), out_shape=jax....  62.7 us
    dot_general x1, matrix products, on_device(): jnp.einsum('rc,dc->rd', back_vertical, loc_horizontal, preferred_element_...  3.84 us

profile of v8, /device:TPU:6, one launch (start us, length us, event | category | flops | bytes accessed | tf_op | source)
XLA Modules:
  0.0 66.5 jit_solution(10626181387630223789)
XLA Ops:
  0.0 0.0 copy-start.1
  0.0 0.0 copy-start
  0.0 62.7 %shard_map.100 = bf16[512,1024]{1,0:T(8,128)(2,1)} custom-call(s32[256]{0:T(256)} %block_ref.1, s32[32]{0:T(128)} %count_ref.1, f32[64,64]{1,0:T(8,128)} %loc_vertical_ref.1, f32[256,128]{1,0:T(8,128)} %innov_ref.1, f32[256,128]{1,0:T(8,128)} %prec_ref.1, bf16[8,64,1024]{2,1,0:T(8,128)(2,1)} %pert_hbm.1, f32[8,64,1024]{2,1,0:T(8,128)} %control_hbm.1, ...), custom_call_target="tpu_custom_call" | custom-call | tf_op jit(solution)/shard_map/pallas_call | solution.py:497
  62.7 0.0 copy-done.1
  62.7 0.0 copy-done
  62.7 3.8 %bitcast_add_fusion = f32[512,1024]{1,0:T(8,128)} fusion(f32[8,64,1024]{2,1,0:T(8,128)S(1)} %copy-done, bf16[512,1024]{1,0:T(8,128)(2,1)} %shard_map.100, bf16[1024,1024]{1,0:T(8,128)(2,1)S(1)} %copy-done.1), kind=kOutput, calls=%fused_computation | convolution fusion | flops 1074790400 | bytes 7340032 | tf_op jit(solution)/shard_map/rc,dc->rd/dot_general | solution.py:578
Async XLA Ops:
  0.0 62.7 %copy-start.1 = (bf16[1024,1024]{1,0:T(8,128)(2,1)S(1)}, bf16[1024,1024]{1,0:T(8,128)(2,1)}, u32[]{:S(2)}) copy-start(bf16[1024,1024]{1,0:T(8,128)(2,1)} %horizontal_hbm.1) | copy-start | bytes 6291460
  0.0 62.7 %copy-start = (f32[8,64,1024]{2,1,0:T(8,128)S(1)}, f32[8,64,1024]{2,1,0:T(8,128)}, u32[]{:S(2)}) copy-start(f32[8,64,1024]{2,1,0:T(8,128)} %control_hbm.1) | copy-start | bytes 6291460

commit v9 on v8

--- a/solution.py
+++ b/solution.py
@@ -222,17 +222,11 @@
             last_ref[base + k] = latest
         return carry
 
-    lv = loc_vertical_ref[...]
-    head = lv.astype(BF16)
-    heads = jnp.concatenate([head, (lv - head.astype(F32)).astype(BF16)], axis=0)
+    lv = loc_vertical_ref[...].astype(BF16)
     first_loads[0].wait()
 
     def one_member(k, carry):
-        field = control[k]
-        field_head = field.astype(BF16)
-        field_rest = (field - field_head.astype(F32)).astype(BF16)
-        two = jnp.dot(heads, field_head, preferred_element_type=F32)
-        sum_ = two[:64] + two[64:] + jnp.dot(head, field_rest, preferred_element_type=F32)
+        sum_ = jnp.dot(lv, control[k].astype(BF16), preferred_element_type=F32)
         localized[pl.ds(pl.multiple_of(k * 64, 64), 64), :] = sum_.astype(BF16)
         return carry
 
@@ -450,9 +444,7 @@
             sum_ = sum_ + unit_in[q, h].astype(F32)
         final[2 * e + h] = sum_.astype(BF16)
     go(("ug", 1), ("ug", 3), ("ug", 2))
-    lv_t = loc_vertical_ref[...].T
-    head_t = lv_t.astype(BF16)
-    heads_t = jnp.concatenate([head_t, (lv_t - head_t.astype(F32)).astype(BF16)], axis=0)
+    lv_t = loc_vertical_ref[...].T.astype(BF16)
     for q in (0, 1, 3, 2):
         if q > 0:
             got(("ug", (4 - q)))
@@ -463,10 +455,7 @@
         )
         for k in range(8):
             field = pert[k, :, at].astype(F32) * adjoint
-            field_head = field.astype(BF16)
-            field_rest = (field - field_head.astype(F32)).astype(BF16)
-            two = jnp.dot(heads_t, field_head, preferred_element_type=F32)
-            sum_ = two[:64] + two[64:] + jnp.dot(head_t, field_rest, preferred_element_type=F32)
+            sum_ = jnp.dot(lv_t, field.astype(BF16), preferred_element_type=F32)
             out_ref[k * 64 : (k + 1) * 64, at] = sum_.astype(BF16)
     for name in ways:
         copy_of(name).wait_send()

time: 67 us -> 66.1 us (0.987)
  Pallas kernels: 62.7 us -> 61.9 us
    pallas_call x1, Pallas kernels: 62.7 us -> 61.9 us  [exchange(): pl.pallas_call(functools.partial(exchange_kernel, factor), out_shape=jax....]
where the time goes in v9:
time: 66.1 us; the launch traced here: 65.7 us
  Pallas kernels  61.9 us (94%)
  matrix products  3.84 us (6%)
    pallas_call x1, Pallas kernels, exchange(): pl.pallas_call(functools.partial(exchange_kernel, factor), out_shape=jax....  61.9 us
    dot_general x1, matrix products, on_device(): jnp.einsum('rc,dc->rd', back_vertical, loc_horizontal, preferred_element_...  3.84 us

profile of v9, /device:TPU:6, one launch (start us, length us, event | category | flops | bytes accessed | tf_op | source)
XLA Modules:
  0.0 65.7 jit_solution(703031417662390823)
XLA Ops:
  0.0 0.0 copy-start.1
  0.0 0.0 copy-start
  0.0 61.9 %shard_map.100 = bf16[512,1024]{1,0:T(8,128)(2,1)} custom-call(s32[256]{0:T(256)} %block_ref.1, s32[32]{0:T(128)} %count_ref.1, f32[64,64]{1,0:T(8,128)} %loc_vertical_ref.1, f32[256,128]{1,0:T(8,128)} %innov_ref.1, f32[256,128]{1,0:T(8,128)} %prec_ref.1, bf16[8,64,1024]{2,1,0:T(8,128)(2,1)} %pert_hbm.1, f32[8,64,1024]{2,1,0:T(8,128)} %control_hbm.1, ...), custom_call_target="tpu_custom_call" | custom-call | tf_op jit(solution)/shard_map/pallas_call | solution.py:486
  61.9 0.0 copy-done.1
  61.9 0.0 copy-done
  61.9 3.8 %bitcast_add_fusion = f32[512,1024]{1,0:T(8,128)} fusion(f32[8,64,1024]{2,1,0:T(8,128)S(1)} %copy-done, bf16[512,1024]{1,0:T(8,128)(2,1)} %shard_map.100, bf16[1024,1024]{1,0:T(8,128)(2,1)S(1)} %copy-done.1), kind=kOutput, calls=%fused_computation | convolution fusion | flops 1074790400 | bytes 7340032 | tf_op jit(solution)/shard_map/rc,dc->rd/dot_general | solution.py:567
Async XLA Ops:
  0.0 61.9 %copy-start.1 = (bf16[1024,1024]{1,0:T(8,128)(2,1)S(1)}, bf16[1024,1024]{1,0:T(8,128)(2,1)}, u32[]{:S(2)}) copy-start(bf16[1024,1024]{1,0:T(8,128)(2,1)} %horizontal_hbm.1) | copy-start | bytes 6291460
  0.0 61.9 %copy-start = (f32[8,64,1024]{2,1,0:T(8,128)S(1)}, f32[8,64,1024]{2,1,0:T(8,128)}, u32[]{:S(2)}) copy-start(f32[8,64,1024]{2,1,0:T(8,128)} %control_hbm.1) | copy-start | bytes 6291460

commit v10 on v9

--- a/solution.py
+++ b/solution.py
@@ -24,16 +24,12 @@
     (3, 3), (1, 3), (3, 2), (1, 2), (2, 0), (2, 1), (2, 3), (2, 2),
 )
 ARRIVE = {
-    1: (
-        (0, 0, 3), (0, 0, 1), (1, 0, 3), (1, 0, 1),
-        (0, 3, 0), (0, 1, 0), (1, 3, 0), (1, 1, 0),
-    ),
-    3: ((1, 0, 2),),
+    1: ((0, 0, 3), (0, 0, 1), (1, 0, 3), (1, 0, 1), (0, 3, 0), (0, 1, 0), (1, 3, 0), (1, 1, 0)),
+    4: ((1, 0, 2),),
     5: ((0, 3, 3), (0, 1, 1), (0, 3, 1), (0, 1, 3), (1, 3, 1), (1, 1, 1)),
     7: ((1, 3, 3), (1, 1, 3)),
-    8: ((0, 3, 2), (0, 1, 2)),
-    9: ((1, 3, 2), (1, 1, 2)),
-    10: ((1, 2, 0),),
+    9: ((0, 3, 2), (0, 1, 2), (1, 3, 2), (1, 1, 2)),
+    11: ((1, 2, 0),),
     12: ((1, 2, 1),),
     13: ((1, 2, 3),),
     14: ((1, 2, 2),),
@@ -536,6 +532,35 @@
     )
 
 
+def spread_kernel(factor, control_ref, back_ref, horizontal_ref, out_ref):
+    spread = lax.dot_general(
+        back_ref[...],
+        horizontal_ref[...],
+        (((1,), (1,)), ((), ())),
+        preferred_element_type=F32,
+    )
+    for k in range(control_ref.shape[0]):
+        out_ref[k] = control_ref[k] + factor * spread[k * 64 : (k + 1) * 64]
+
+
+def add_spread(factor, control, back_vertical, loc_horizontal):
+    members, levels, columns = control.shape
+    width = 512
+    chunk = pl.BlockSpec((members, levels, width), lambda i: (0, 0, i))
+    return pl.pallas_call(
+        functools.partial(spread_kernel, factor),
+        grid=(columns // width,),
+        out_shape=jax.ShapeDtypeStruct(control.shape, F32),
+        in_specs=[
+            chunk,
+            pl.BlockSpec(back_vertical.shape, lambda i: (0, 0)),
+            pl.BlockSpec((width, columns), lambda i: (i, 0)),
+        ],
+        out_specs=chunk,
+        compiler_params=pltpu.CompilerParams(vmem_limit_bytes=24 * 1024 * 1024),
+    )(control, back_vertical, loc_horizontal)
+
+
 def on_device(
     perturbations,
     control,
@@ -564,11 +589,7 @@
         obs_weight,
         obs_vertical,
     )
-    spread_back = jnp.einsum(
-        "rc,dc->rd", back_vertical, loc_horizontal, preferred_element_type=F32
-    )
-    flat_control = control.reshape(members_dev * levels, columns)
-    return (flat_control + factor * spread_back).reshape(control.shape)
+    return add_spread(factor, control, back_vertical, loc_horizontal)
 
 
 def solution(mesh):

time: 66.1 us -> 66.2 us (level)
  matrix products: 3.84 us -> 0 us
  Pallas kernels: 61.9 us -> 64.8 us
  local copies, waits for them, and re-layouts: 0.01 us -> 1.23 us
    dot_general x1 -> x0, matrix products: 3.84 us -> none  [on_device(): jnp.einsum('rc,dc->rd', back_vertical, loc_horizontal, preferred_element_...]
    pallas_call x0 -> x1, Pallas kernels: none -> 2.64 us  [add_spread(): pl.pallas_call(functools.partial(spread_kernel, factor), grid=(columns //...]
    unnamed x4 -> x6, local copies, waits for them, and re-layouts: 0.01 us -> 1.23 us
where the time goes in v10:
time: 66.2 us; the launch traced here: 66.1 us
  Pallas kernels  64.8 us (98%)
  local copies, waits for them, and re-layouts  1.23 us (2%)
    pallas_call x1, Pallas kernels, exchange(): pl.pallas_call(functools.partial(exchange_kernel, factor), out_shape=jax....  62.2 us
    pallas_call x1, Pallas kernels, add_spread(): pl.pallas_call(functools.partial(spread_kernel, factor), grid=(columns //...  2.64 us

profile of v10, /device:TPU:6, one launch (start us, length us, event | category | flops | bytes accessed | tf_op | source)
XLA Modules:
  0.0 66.1 jit_solution(6736849504437974707)
XLA Ops:
  0.0 0.0 copy-start.1
  0.0 0.0 copy-start
  0.0 62.2 %shard_map.100.back_ref = bf16[512,1024]{1,0:T(8,128)(2,1)} custom-call(s32[256]{0:T(256)} %block_ref.1, s32[32]{0:T(128)} %count_ref.1, f32[64,64]{1,0:T(8,128)} %loc_vertical_ref.1, f32[256,128]{1,0:T(8,128)} %innov_ref.1, f32[256,128]{1,0:T(8,128)} %prec_ref.1, bf16[8,64,1024]{2,1,0:T(8,128)(2,1)} %pert_hbm.1, f32[8,64,1024]{2,1,0:T(8,128)} %control_ref.1, ...), custom_call_target="tpu_custom_call" | custom-call | tf_op jit(solution)/shard_map/pallas_call | solution.py:482
  62.2 0.0 copy-done.1
  62.2 0.0 copy-done
  62.2 0.0 copy-start.2
  62.2 1.2 %copy-done.2 = bf16[512,1024]{1,0:T(8,128)(2,1)S(1)} copy-done((bf16[512,1024]{1,0:T(8,128)(2,1)S(1)}, bf16[512,1024]{1,0:T(8,128)(2,1)}, u32[]{:S(2)}) %copy-start.2) | copy-done | bytes 1048600
  63.4 2.6 %shard_map.101 = f32[8,64,1024]{2,1,0:T(8,128)} custom-call(f32[8,64,1024]{2,1,0:T(8,128)S(1)} %copy-done, bf16[512,1024]{1,0:T(8,128)(2,1)S(1)} %copy-done.2, bf16[1024,1024]{1,0:T(8,128)(2,1)S(1)} %copy-done.1), custom_call_target="tpu_custom_call" | custom-call | tf_op jit(solution)/shard_map/pallas_call | solution.py:550
Async XLA Ops:
  0.0 62.2 %copy-start.1 = (bf16[1024,1024]{1,0:T(8,128)(2,1)S(1)}, bf16[1024,1024]{1,0:T(8,128)(2,1)}, u32[]{:S(2)}) copy-start(bf16[1024,1024]{1,0:T(8,128)(2,1)} %horizontal_ref.1) | copy-start | bytes 6291460
  0.0 62.2 %copy-start = (f32[8,64,1024]{2,1,0:T(8,128)S(1)}, f32[8,64,1024]{2,1,0:T(8,128)}, u32[]{:S(2)}) copy-start(f32[8,64,1024]{2,1,0:T(8,128)} %control_ref.1) | copy-start | bytes 6291460
  62.2 1.2 %copy-start.2 = (bf16[512,1024]{1,0:T(8,128)(2,1)S(1)}, bf16[512,1024]{1,0:T(8,128)(2,1)}, u32[]{:S(2)}) copy-start(bf16[512,1024]{1,0:T(8,128)(2,1)} %shard_map.100.back_ref) | copy-start | bytes 3145732
